TPU v7x, 32 devices: a whole 2x2x4 slice. The times are simulated.
32 devices in a mesh: seq: 8 (over y, x, core), head: 4 (over z).
Axes of the slice: x: 2, y: 2, z: 4, core: 2. Of those that a mesh axis runs over, the one named last changes fastest.
Arguments:
- tokens: bfloat16 [1, 4096, 1536], P(None, 'seq', 'head'), may hold values from -6 to 6
- decay_codes: int32 [1, 4096, 48], P(None, 'seq', 'head'), may hold values from 0 to 524288, as said below
- norm_gain: bfloat16 [1536], P('head'), may hold values from 0.25 to 1.75
- gate_weight: bfloat16 [1536, 3072], P(None, 'head'), may hold values from -0.15625 to 0.15625
- value_weight: bfloat16 [1536, 3072], P(None, 'head'), may hold values from -0.15625 to 0.15625
- state_weight: bfloat16 [1536, 256], replicated, may hold values from -0.15625 to 0.15625
- value_kernel: bfloat16 [4, 3072], P(None, 'head'), may hold values from -3 to 3
- value_bias: bfloat16 [3072], P('head'), may hold values from -3 to 3
- state_kernel: bfloat16 [4, 256], replicated, may hold values from -3 to 3
- state_bias: bfloat16 [256], replicated, may hold values from -3 to 3
- skip_scale: float32 [48], P('head'), may hold values from 0.5 to 1.5
- gated_gain: bfloat16 [3072], P('head'), may hold values from 0.25 to 1.75
- output_weight: bfloat16 [3072, 1536], P('head'), may hold values from -0.109375 to 0.109375
- cotangent: bfloat16 [1, 4096, 1536], P(None, 'seq', 'head'), may hold values from -6 to 6
Outputs:
- block_out: bfloat16 [1, 4096, 1536], P(None, 'seq', 'head')
- tokens_gradient: bfloat16 [1, 4096, 1536], P(None, 'seq', 'head')
- norm_gain_gradient: float32 [1536], P('head')
- gate_weight_gradient: float32 [1536, 3072], P(None, 'head')
- value_weight_gradient: float32 [1536, 3072], P(None, 'head')
- state_weight_gradient: float32 [1536, 256], replicated
- value_kernel_gradient: float32 [4, 3072], P(None, 'head')
- value_bias_gradient: float32 [3072], P('head')
- state_kernel_gradient: float32 [4, 256], replicated
- state_bias_gradient: float32 [256], replicated
- skip_scale_gradient: float32 [48], P('head')
- gated_gain_gradient: float32 [3072], P('head')
- output_weight_gradient: float32 [3072, 1536], P('head')
Inputs may be any that keep to these rules, and one draw needn't show every extreme that they name: `decay_codes`: decay factors are exp(-code / 1048576).
All inputs are finite; a program needn't handle non-finite values.
Results may differ from a plain program's by a relative error of at most 0.012.
The roundings to bfloat16 on the way count: a program that leaves them out, or rounds other values in their place, can miss the bound.
Values may be sent and summed in bfloat16 or wider, within the bound.
No kernel may reach another device: no remote copies, remote signals or barrier semaphores. Data moves between devices by JAX's collectives and lax.ppermute only.
A program may use at most 128 MiB of HBM per device.

v0:
```python
import functools

import jax
import jax.numpy as jnp
from jax import lax
from jax.experimental import pallas as pl
from jax.experimental.pallas import tpu as pltpu
from jax.sharding import Mesh
from jax.sharding import PartitionSpec as P

HEAD_DIM = 64
NSTATE = 128
KERNEL = 4
CHUNK = 128
BLOCK = 384
VMEM_LIMIT = 20 * 1024 * 1024
HALO = 16


DECAY_STEP = 1.0 / 1048576.0
EPSILON = 1e-05
BF16 = jnp.bfloat16
F32 = jnp.float32


def from_behind(value, by):
    axis = ("chip", "core")
    size = lax.axis_size("chip") * 2
    pairs = [(i, i + by) for i in range(size) if 0 <= i + by < size]
    return lax.ppermute(value, axis, pairs)


def beside(value):
    return lax.ppermute(value, "core", [(0, 1), (1, 0)])


def turn(value, axis, by):
    size = lax.axis_size(axis)
    return lax.ppermute(value, axis, [(i, (i + by) % size) for i in range(size)])


def turn_all(value, axis):
    return [value] + [turn(value, axis, by) for by in range(1, lax.axis_size(axis))]


def line_parts(value, axis):
    if lax.axis_size(axis) != 4:
        return turn_all(value, axis), value
    two = turn(value, axis, 2)
    one = lax.ppermute(value, axis, [(0, 1), (1, 2), (2, 3)])
    three = lax.ppermute(value, axis, [(1, 0), (2, 1), (3, 2)])
    passed = lax.ppermute(two, axis, [(2, 3), (1, 0)])
    return [value, one, two, three], passed


def deal(parts, axis):
    return lax.all_to_all(parts, axis, 0, 0)


def cross(value, bits):
    return lax.ppermute(value, "chip", [(i, i ^ bits) for i in range(lax.axis_size("chip"))])


def cross_all(value):
    return [value] + [cross(value, bits) for bits in range(1, lax.axis_size("chip"))]


def butterfly(value, axis):
    bits = 1
    while bits < lax.axis_size(axis):
        size = lax.axis_size(axis)
        value = value + lax.ppermute(value, axis, [(i, i ^ bits) for i in range(size)])
        bits *= 2
    return value


def decay_weights(logs, backward):
    chips, mine = lax.axis_size("chip"), lax.axis_index("chip")
    source = (jnp.arange(chips) ^ mine)[:, None]
    middle = jnp.arange(chips)[None, :]
    if backward:
        between, passes = (middle < source) & (middle > mine), source > mine
    else:
        between, passes = (middle > source) & (middle < mine), source < mine
    spans = jnp.sum(jnp.where(between[:, :, None], logs[None], 0.0), axis=1)
    return jnp.where(passes, jnp.exp(spans), 0.0)


def entering(total, own_decay, other_decay, weights, backward):
    core = lax.axis_index("core")
    receives = core == (0 if backward else 1)
    half = total.shape[0] // 2
    partner = beside(total)
    part = lambda value: lax.dynamic_slice_in_dim(value, core * half, half, 0)
    pair = jnp.where(
        receives,
        own_decay * part(partner) + part(total),
        other_decay * part(total) + part(partner),
    )
    prefix = jnp.zeros_like(pair)
    for bits in range(1, lax.axis_size("chip")):
        prefix = prefix + cross(pair, bits) * weights[bits : bits + 1]
    other = beside(prefix)
    whole = jnp.where(
        core == 0,
        jnp.concatenate([prefix, other], axis=0),
        jnp.concatenate([other, prefix], axis=0),
    )
    return jnp.where(receives, other_decay * whole + partner, whole), pair


def sum_pieces(chip, kept, given, cut, paired, name):
    chips, rows, channels = kept.shape
    arrived = beside(given)
    rest = rows - cut
    size = chips * rows * channels
    if chips != 4:
        halves = run(
            functools.partial(half_kernel, paired, chips), name + "_half", size,
            [chip, (WHOLE, kept), (WHOLE, arrived)],
            [(WHOLE, (rows, channels), F32)] + [(WHOLE, (rows, channels), BF16)] * (chips - 1),
        )
        parts = [halves[0]] + [cross(halves[bits], bits) for bits in range(1, chips)]
        first, last = run(
            functools.partial(piece_kernel, chips, paired, cut), name + "_piece", size,
            [(WHOLE, part) for part in parts],
            [(WHOLE, (cut, channels), BF16), (WHOLE, (rest, channels), F32 if paired else BF16)],
        )
        return first, last, halves[0]
    first, first_give, last, last_give = run(
        functools.partial(square_half_kernel, paired), name + "_half", size,
        [chip, (WHOLE, kept), (WHOLE, arrived)],
        [
            (WHOLE, (2, cut, channels), F32), (WHOLE, (2, cut, channels), BF16),
            (WHOLE, (2, rest, channels), F32), (WHOLE, (2, rest, channels), BF16),
        ],
    )
    mark = first
    first, first_give, last, last_give = run(
        functools.partial(square_next_kernel, paired), name + "_next", size,
        [
            (WHOLE, first), (WHOLE, cross(first_give, 1)),
            (WHOLE, last), (WHOLE, cross(last_give, 2)),
        ],
        [
            (WHOLE, (cut, channels), F32), (WHOLE, (cut, channels), BF16),
            (WHOLE, (rest, channels), F32), (WHOLE, (rest, channels), BF16),
        ],
    )
    first, last = run(
        functools.partial(square_last_kernel, paired), name + "_piece", size,
        [
            (WHOLE, first), (WHOLE, cross(first_give, 2)),
            (WHOLE, last), (WHOLE, cross(last_give, 1)),
        ],
        [(WHOLE, (cut, channels), BF16), (WHOLE, (rest, channels), F32 if paired else BF16)],
    )
    return first, last, mark


def collect(piece, order):
    chips = lax.axis_size("chip")
    if chips != 4:
        found = [(value[None], (bits,)) for bits, value in enumerate(cross_all(piece))]
    else:
        near, far = order
        both = jnp.stack([piece, cross(piece, near)])
        found = [(both, (0, near)), (cross(both, far), (far, far ^ near))]
    return [(value, beside(value), bits) for value, bits in found]


def dot(left, right):
    return jnp.dot(left, right, preferred_element_type=F32)


def dot_nt(left, right):
    return lax.dot_general(left, right, (((1,), (1,)), ((), ())), preferred_element_type=F32)


def dot_tn(left, right):
    return lax.dot_general(left, right, (((0,), (0,)), ((), ())), preferred_element_type=F32)


def split(values):
    high = values.astype(BF16)
    return high, (values - high.astype(F32)).astype(BF16)


def lower_mask():
    row = lax.broadcasted_iota(jnp.int32, (CHUNK, CHUNK), 0)
    column = lax.broadcasted_iota(jnp.int32, (CHUNK, CHUNK), 1)
    return row >= column


def decay_kernel(codes_ref, weight_ref, e_ref, f_ref, k_ref):
    heads, channels = codes_ref.shape[1], e_ref.shape[1]
    row = lax.broadcasted_iota(jnp.int32, (heads, channels), 0)
    column = lax.broadcasted_iota(jnp.int32, (heads, channels), 1)
    first = row * HEAD_DIM
    spread = jnp.where((column >= first) & (column < first + HEAD_DIM), 1.0, 0.0).astype(BF16)

    def expand(values):
        high, low = split(values)
        return dot(high, spread) + dot(low, spread)

    lower = jnp.where(lower_mask(), 1.0, 0.0).astype(F32)
    count = codes_ref.shape[0] // CHUNK
    line = lax.broadcasted_iota(jnp.int32, (8, heads), 0)
    marks = jnp.zeros((8, heads), F32)
    total = jnp.zeros((1, heads), F32)
    for chunk in range(count):
        rows = pl.ds(chunk * CHUNK, CHUNK)
        logs = codes_ref[rows, :].astype(F32) * (-DECAY_STEP)
        cumulative = jnp.dot(
            lower, logs, precision=lax.Precision.HIGHEST, preferred_element_type=F32
        )
        last = cumulative[CHUNK - 1 :]
        middle = 0.5 * last
        e_ref[rows, :] = expand(jnp.exp(cumulative - middle))
        f_ref[rows, :] = expand(weight_ref[rows, :] * jnp.exp(middle - cumulative))
        marks = jnp.where(line == chunk, jnp.exp(middle), marks)
        total = total + last
    marks = jnp.where(line == 7, total, marks)
    high, low = split(marks)
    lowest = (marks - high.astype(F32) - low.astype(F32)).astype(BF16)
    k_ref[...] = dot(high, spread) + dot(low, spread) + dot(lowest, spread)


def taps(window, kernel, bias, begin):
    summed = bias
    for offset in range(KERNEL):
        summed = summed + kernel[offset : offset + 1] * window[begin + offset : begin + offset + CHUNK]
    return summed


def silu_parts(values):
    sigmoid = jax.nn.sigmoid(values)
    return values * sigmoid, sigmoid * (1.0 + values * (1.0 - sigmoid))


def first_step(action):
    pl.when(pl.program_id(0) == 0)(action)


def clear(*refs):
    def action():
        for ref in refs:
            ref[...] = jnp.zeros_like(ref)

    first_step(action)


def place_parts(mine, parts, target, width, value):
    size = len(parts)
    if width % 128 == 0:
        for i in range(size):
            owner = lax.rem(mine + size - i, size)
            target[:, pl.ds(pl.multiple_of(owner * width, 128), width)] = value(i)
        return

    def write(me):
        for i in range(size):
            owner = (me + size - i) % size
            target[:, owner * width : (owner + 1) * width] = value(i)

    for me in range(size):
        pl.when(mine == me)(functools.partial(write, me))


def norm_kernel(size, head_ref, passed_ref, *refs):
    parts, margins, (own_ref,) = refs[:size], refs[size : 2 * size], refs[2 * size : 2 * size + 1]
    normed_ref, full_ref, gain_ref, scale_ref, copy_ref = refs[2 * size + 1 : 2 * size + 6]
    head_normed, = refs[2 * size + 6 :]
    width = parts[0].shape[1]
    mine = head_ref[0]

    def part(i):
        if size == 4 and i == 1:
            return jnp.where(mine == 0, passed_ref[...], parts[i][...])
        if size == 4 and i == 3:
            return jnp.where(mine == 3, passed_ref[...], parts[i][...])
        return parts[i][...]

    def scale_of(values):
        squares = sum(jnp.sum(value.astype(F32) ** 2, axis=1, keepdims=True) for value in values)
        return lax.rsqrt(squares / (size * width) + EPSILON)

    scale = scale_of(part(i) for i in range(size))
    scale_ref[...] = jnp.broadcast_to(scale, scale_ref.shape)
    ahead = scale_of(ref[:HALO] for ref in margins)
    gain = lambda i: margins[i][HALO : HALO + 1, :].astype(F32)
    place_parts(
        mine, margins, head_normed, width,
        lambda i: (margins[i][:HALO].astype(F32) * ahead * gain(i)).astype(BF16),
    )
    place_parts(
        mine, parts, normed_ref.at[HALO:], width,
        lambda i: (part(i).astype(F32) * scale_ref[:, 0:1] * gain(i)).astype(BF16),
    )
    normed_ref[:HALO, :] = head_normed[...]
    place_parts(mine, parts, full_ref, width, part)
    place_parts(
        mine, margins, gain_ref, width, lambda i: jnp.broadcast_to(gain(i), (8, width))
    )
    for i in range(size):
        copy_ref[i] = own_ref[...]


def place_kernel(parts_ref, target):
    width = parts_ref.shape[2]
    for i in range(parts_ref.shape[0]):
        target[:, i * width : (i + 1) * width] = parts_ref[i]


def conv_kernel(
    value_ref, state_ref, value_kernel_ref, value_bias_ref, state_kernel_ref, state_bias_ref,
    f_ref, k_ref, conv_ref, weighted_ref, value_slope_ref, maps_ref, state_slope_ref, total_ref,
):
    chunk = pl.program_id(0)
    clear(total_ref)
    around = pl.ds(pl.multiple_of(chunk * CHUNK, CHUNK), CHUNK + HALO)
    pre = taps(
        state_ref[around, :].astype(F32), state_kernel_ref[...].astype(F32),
        state_bias_ref[...].astype(F32), HALO - KERNEL + 1,
    )
    conv, slope = silu_parts(pre)
    maps = conv.astype(BF16)
    maps_ref[...] = maps
    state_slope_ref[...] = slope
    pre = taps(
        value_ref[around, :].astype(F32), value_kernel_ref[...].astype(F32),
        value_bias_ref[...].astype(F32), HALO - KERNEL + 1,
    )
    conv, slope = silu_parts(pre)
    conv = conv.astype(BF16)
    conv_ref[...] = conv
    value_slope_ref[...] = slope
    weighted = (conv.astype(F32) * f_ref[...]).astype(BF16)
    weighted_ref[...] = weighted
    factor = k_ref[pl.ds(chunk, 1), :]
    total_ref[...] = factor * (factor * total_ref[...] + dot_tn(maps[:, :NSTATE], weighted))


def mixer_kernel(
    state_in_ref, maps_ref, weighted_ref, conv_ref, e_ref, k_ref, skip_ref, gate_ref, grad_ref, gain_ref,
    mixer_ref, stats_ref, high_ref, low_ref, state_ref,
):
    chunk = pl.program_id(0)

    def start():
        state_ref[...] = state_in_ref[...]

    first_step(start)
    lane = lax.broadcasted_iota(jnp.int32, (CHUNK, CHUNK), 1)
    factor = k_ref[pl.ds(chunk, 1), :]
    input_map, output_map = maps_ref[:, :NSTATE], maps_ref[:, NSTATE:]
    weighted = weighted_ref[...]
    scaled = factor * state_ref[...]
    high, low = split(scaled)
    high_ref[0], low_ref[0] = high, low
    scores = jnp.where(lower_mask(), dot_nt(output_map, input_map), 0.0).astype(BF16)
    mixed = dot(
        jnp.concatenate([scores, output_map], axis=1), jnp.concatenate([weighted, high], axis=0)
    )
    mixed = mixed + dot(output_map, low)
    mixer = e_ref[...] * mixed + skip_ref[...] * conv_ref[...].astype(F32)
    mixer_ref[...] = mixer
    gate = gate_ref[...]
    gated = mixer * (gate * jax.nn.sigmoid(gate))
    squares = jnp.sum(gated * gated, axis=1, keepdims=True)
    products = jnp.sum(gated * (grad_ref[...] * gain_ref[...].astype(F32)), axis=1, keepdims=True)
    sums = jnp.where(lane == 0, squares, jnp.where(lane == 1, products, 0.0))
    stats_ref[...] = sums.T[:8]
    state_ref[...] = factor * (scaled + dot_tn(input_map, weighted))


def column(row_block):
    rest = jnp.zeros((CHUNK - row_block.shape[0], CHUNK), F32)
    return jnp.concatenate([row_block, rest], axis=0).T


def gate_kernel(
    inner, chunks, size, *refs
):
    stats_refs = refs[:size]
    (
        mixer_ref, gate_ref, grad_ref, gain_ref, conv_ref, e_ref, k_ref, maps_ref,
        mixed_ref, gate_grad_ref, mixer_grad_ref, small_ref, total_ref,
    ) = refs[size:]
    chunk = chunks - 1 - pl.program_id(0)
    clear(small_ref, total_ref)
    gain = gain_ref[...].astype(F32)
    stats = column(sum(ref[...] for ref in stats_refs))
    scale = lax.rsqrt(stats[:, 0:1] / inner + EPSILON)
    cross_term = stats[:, 1:2] * (scale * scale * scale) / inner
    silu, slope = silu_parts(gate_ref[...])
    mixer = mixer_ref[...]
    gated = mixer * silu
    normed = gated * scale
    mixed_ref[...] = (normed * gain).astype(BF16)
    grad = grad_ref[...]
    gated_grad = scale * (grad * gain) - gated * cross_term
    gate_grad_ref[...] = (gated_grad * mixer * slope).astype(BF16)
    mixer_grad = gated_grad * silu
    mixer_grad_ref[...] = mixer_grad
    small_ref[0:1, :] += jnp.sum(grad * normed, axis=0, keepdims=True)
    small_ref[1:2, :] += jnp.sum(mixer_grad * conv_ref[...].astype(F32), axis=0, keepdims=True)
    high, low = split(e_ref[...] * mixer_grad)
    output_map = maps_ref[:, NSTATE:]
    factor = k_ref[pl.ds(chunk, 1), :]
    total_ref[...] = factor * (
        factor * total_ref[...] + (dot_tn(output_map, high) + dot_tn(output_map, low))
    )


def back_kernel(
    chunks, early_ref, out_ref, state_in_ref, mixer_grad_ref, e_ref, f_ref, k_ref, weighted_ref, high_ref, low_ref,
    maps_ref, value_slope_ref, state_slope_ref, skip_ref,
    value_ref, map_ref, state_ref,
):
    chunk = chunks - 1 - pl.program_id(0)

    def start():
        state_ref[...] = state_in_ref[...]

    first_step(start)
    lower = lower_mask()
    row = lax.broadcasted_iota(jnp.int32, (CHUNK, CHUNK), 0)
    upper = row <= lax.broadcasted_iota(jnp.int32, (CHUNK, CHUNK), 1)
    factor = k_ref[pl.ds(chunk, 1), :]
    input_map, output_map = maps_ref[:, :NSTATE], maps_ref[:, NSTATE:]
    weighted = weighted_ref[...]
    mixer_grad = mixer_grad_ref[...]
    high, low = split(e_ref[...] * mixer_grad)
    scaled = factor * state_ref[...]
    state_high, state_low = split(scaled)
    both = jnp.concatenate([weighted, high_ref[0]], axis=0)
    sums = dot_nt(high, both) + dot_nt(low, both)
    score_grad = jnp.where(lower, sums[:, :CHUNK], 0.0).astype(BF16)
    output_grad = sums[:, CHUNK:] + dot_nt(high, low_ref[0]) + dot(score_grad, input_map)
    sums = dot_nt(weighted, jnp.concatenate([state_high, state_low], axis=0))
    input_grad = sums[:, :NSTATE] + sums[:, NSTATE:] + dot_tn(score_grad, output_map)
    scores = jnp.where(upper, dot_nt(input_map, output_map), 0.0).astype(BF16)
    grads = dot(
        jnp.concatenate([scores, input_map], axis=1), jnp.concatenate([high, state_high], axis=0)
    )
    value_ref[...] = (f_ref[...] * grads + skip_ref[...] * mixer_grad) * value_slope_ref[...]
    slope = state_slope_ref[...]
    map_ref[:, :NSTATE] = input_grad * slope[:, :NSTATE]
    map_ref[:, NSTATE:] = output_grad * slope[:, NSTATE:]
    state_ref[...] = factor * (scaled + (dot_tn(output_map, high) + dot_tn(output_map, low)))


def conv_back_kernel(
    chunks, other_ref, value_ref, map_ref, after_ref, value_raw_ref, state_raw_ref, value_kernel_ref,
    state_kernel_ref,
    value_grad_ref, state_grad_ref, value_small_ref, state_small_ref, value_next_ref, state_next_ref,
):
    chunk = chunks - 1 - pl.program_id(0)
    channels = value_ref.shape[1]
    clear(value_small_ref, state_small_ref)

    def start():
        value_next_ref[...] = after_ref[:, :channels]
        state_next_ref[...] = after_ref[:, channels:]

    first_step(start)

    def back(slope_ref, next_ref, raw_ref, kernel_ref, grad_ref, small_ref):
        kernel = kernel_ref[...].astype(F32)
        slope = slope_ref[...]
        window = jnp.concatenate([slope, next_ref[...]], axis=0)
        around = pl.ds(pl.multiple_of(chunk * CHUNK, CHUNK), CHUNK + HALO)
        raw = raw_ref[around, :].astype(F32)
        grad = jnp.zeros_like(slope)
        for offset in range(KERNEL):
            back_by = KERNEL - 1 - offset
            grad = grad + kernel[offset : offset + 1] * window[back_by : back_by + CHUNK]
            begin = HALO - KERNEL + 1 + offset
            small_ref[offset : offset + 1, :] += jnp.sum(
                slope * raw[begin : begin + CHUNK], axis=0, keepdims=True
            )
        small_ref[KERNEL : KERNEL + 1, :] += jnp.sum(slope, axis=0, keepdims=True)
        grad_ref[...] = grad.astype(BF16)
        next_ref[...] = slope[:8]

    back(map_ref, state_next_ref, state_raw_ref, state_kernel_ref, state_grad_ref, state_small_ref)
    back(value_ref, value_next_ref, value_raw_ref, value_kernel_ref, value_grad_ref, value_small_ref)


def out_kernel(pair_ref, mixed_ref, weight_ref, out_ref):
    width = out_ref.shape[2]
    for owner in range(out_ref.shape[0]):
        value = dot(mixed_ref[...], weight_ref[:, owner * width : (owner + 1) * width])
        out_ref[owner] = value.astype(BF16)


def normed_kernel(
    late_ref, gate_grad_ref, value_grad_ref, state_grad_ref, gate_weight_ref, value_weight_ref,
    state_weight_ref, full_ref, gain_ref, out_ref
):
    size, _, width = out_ref.shape
    count = full_ref.shape[0]
    crossed = jnp.zeros((count, 1), F32)
    for owner in range(size):
        own = slice(owner * width, (owner + 1) * width)
        value = (
            dot_nt(gate_grad_ref[...], gate_weight_ref[own, :])
            + dot_nt(value_grad_ref[...], value_weight_ref[own, :])
            + dot_nt(state_grad_ref[...], state_weight_ref[own, :])
        )
        weighed = value * full_ref[:, own].astype(F32) * gain_ref[0:1, own]
        crossed = crossed + jnp.sum(weighed, axis=1, keepdims=True)
        out_ref[owner, :count, :] = value.astype(BF16)

    chunks = count // CHUNK
    line = lax.broadcasted_iota(jnp.int32, (HALO, CHUNK), 0)
    lane = lax.broadcasted_iota(jnp.int32, (CHUNK, CHUNK), 1)
    packed = jnp.zeros((HALO, CHUNK), F32)
    for chunk in range(chunks):
        sums = crossed[chunk * CHUNK : (chunk + 1) * CHUNK]
        row = jnp.where(lane == 0, sums, 0.0).T[0:1]
        high = row.astype(BF16).astype(F32)
        packed = jnp.where(line == chunk, high, packed)
        packed = jnp.where(line == chunks + chunk, row - high, packed)
    for owner in range(size):
        out_ref[owner, count:, :] = jnp.zeros((HALO, width), BF16)
        out_ref[owner, count:, :CHUNK] = packed.astype(BF16)


def last_kernel(full_width, loose_ref, parts_ref, tokens_ref, scale_ref, gain_ref, cotangent_ref, out_ref):
    count = tokens_ref.shape[0]
    chunks = count // CHUNK
    size = parts_ref.shape[0]
    crossed = sum(parts_ref[i, count:, :CHUNK].astype(F32) for i in range(size))
    crossed = crossed[:chunks] + crossed[chunks : 2 * chunks]
    for chunk in range(chunks):
        rows = slice(chunk * CHUNK, (chunk + 1) * CHUNK)
        normed_grad = sum(parts_ref[i, rows, :].astype(F32) for i in range(size))
        scale = scale_ref[rows, 0:1]
        total = column(jnp.broadcast_to(crossed[chunk : chunk + 1], (8, CHUNK)))[:, 0:1]
        out_ref[rows, :] = (
            scale * gain_ref[...].astype(F32) * normed_grad
            - tokens_ref[rows, :].astype(F32) * (scale * scale * scale * total / full_width)
            + cotangent_ref[rows, :].astype(F32)
        ).astype(BF16)


def store_piece(core_ref, kept_ref, given_ref, place, piece):
    chips = kept_ref.shape[0]
    core, chip = divmod(place, chips)
    piece = piece.astype(BF16)

    @pl.when(core_ref[0] == core)
    def _():
        kept_ref[chip] = piece

    @pl.when(core_ref[0] != core)
    def _():
        given_ref[chip] = piece


def gain_row(weight, block):
    sums = jnp.sum(weight.astype(F32) * block, axis=1, keepdims=True)
    lane = lax.broadcasted_iota(jnp.int32, (CHUNK, CHUNK), 1)
    rows = [
        jnp.where(lane == 0, sums[i : i + CHUNK], 0.0).T[0:1] for i in range(0, BLOCK, CHUNK)
    ]
    return jnp.concatenate(rows, axis=1)


def early_kernel(
    pair_ref, core_ref, normed_ref, gate_ref, mixed_ref, grad_ref, weight_ref,
    kept_ref, given_ref, gain_ref, held_ref
):
    chips, rows, channels = kept_ref.shape
    width = normed_ref.shape[1]
    pieces = 2 * chips
    step = width // pieces
    out_rows = channels // pieces
    for begin in range(0, channels, BLOCK):
        held_ref[begin : begin + BLOCK, :] = dot_tn(mixed_ref[:, begin : begin + BLOCK], grad_ref[...])
    for begin in range(0, width, BLOCK):
        block = dot_tn(normed_ref[HALO:, begin : begin + BLOCK], gate_ref[...])
        gain_ref[0:1, begin : begin + BLOCK] = gain_row(weight_ref[begin : begin + BLOCK, :], block)
        for place in range(begin // step, (begin + BLOCK) // step):
            own = held_ref[place * out_rows : (place + 1) * out_rows, :]
            parts = [block[place * step - begin : (place + 1) * step - begin]]
            parts += [own[:, i : i + channels] for i in range(0, width, channels)]
            store_piece(core_ref, kept_ref, given_ref, place, jnp.concatenate(parts, axis=0))


def late_kernel(
    core_ref, normed_ref, value_ref, state_ref, value_small_ref, gate_small_ref, gain_ref,
    state_small_ref, value_weight_ref, state_weight_ref, gain_full_ref,
    kept_ref, given_ref, own_ref, shared_ref, gains_ref, blocks_ref,
):
    chips, rows, channels = kept_ref.shape
    width, maps_width = normed_ref.shape[1], state_ref.shape[1]
    pieces = 2 * chips
    step = width // pieces
    lanes = channels // 128
    own_ref[...] = jnp.zeros_like(own_ref)
    own_ref[: KERNEL + 1, :] = value_small_ref[: KERNEL + 1, :]
    own_ref[KERNEL + 1 : KERNEL + 3, :] = gate_small_ref[:2, :]
    for begin in range(0, width, BLOCK):
        block = slice(begin, begin + BLOCK)
        columns = normed_ref[HALO:, block]
        value = dot_tn(columns, value_ref[...])
        state = dot_tn(columns, state_ref[...])
        blocks_ref[block, :channels] = value
        blocks_ref[block, channels:] = state
        gains_ref[0:1, block] = (
            gain_ref[0:1, block]
            + gain_row(value_weight_ref[block, :], value)
            + gain_row(state_weight_ref[block, :], state)
        ) / gain_full_ref[0:1, block]
    shared_ref[...] = jnp.zeros_like(shared_ref)
    for i in range(width // channels):
        shared_ref[i : i + 1, :] = gains_ref[0:1, i * channels : (i + 1) * channels]
    begin = width // channels
    for i in range(0, (KERNEL + 1) * maps_width, 128):
        tap, column_from = divmod(i, maps_width)
        row, column_to = divmod(i, channels)
        shared_ref[begin + row : begin + row + 1, column_to : column_to + 128] = state_small_ref[
            tap : tap + 1, column_from : column_from + 128
        ]
    line = lax.broadcasted_iota(jnp.int32, (HALO, channels), 0)
    part = 2 * step // lanes
    for place in range(pieces):
        piece = blocks_ref[place * step : (place + 1) * step, :]
        state = piece[:, channels:]
        stacked = jnp.concatenate([state[:, :128], state[:, 128:]], axis=0)
        stacked = jnp.concatenate(
            [stacked[i * part : (i + 1) * part] for i in range(lanes)], axis=1
        )
        own, shared = own_ref[place : place + 1, :], shared_ref[place : place + 1, :]
        own_high, shared_high = (v.astype(BF16).astype(F32) for v in (own, shared))
        small = jnp.zeros((HALO, channels), F32)
        for at, line_value in enumerate((own_high, own - own_high, shared_high, shared - shared_high)):
            small = jnp.where(line == at, line_value, small)
        store_piece(
            core_ref, kept_ref, given_ref, place,
            jnp.concatenate([piece[:, :channels], stacked, small], axis=0),
        )


def merge_pairs(block):
    tail = block[-HALO:]
    line = lax.broadcasted_iota(jnp.int32, tail.shape, 0)
    own, shared = tail[0:1] + tail[1:2], tail[2:3] + tail[3:4]
    own_high, shared_high = own.astype(BF16).astype(F32), shared.astype(BF16).astype(F32)
    new = jnp.zeros_like(tail)
    for at, value in enumerate((own_high, own - own_high, shared_high, shared - shared_high)):
        new = jnp.where(line == at, value, new)
    return jnp.concatenate([block[:-HALO], new], axis=0)


def half_kernel(paired, chips, chip_ref, kept_ref, arrived_ref, *outs):
    for bits in range(chips):
        place = lax.bitwise_xor(chip_ref[0], bits)
        value = kept_ref[place].astype(F32) + arrived_ref[place].astype(F32)
        if paired:
            value = merge_pairs(value)
        outs[bits][...] = value.astype(outs[bits].dtype)


def piece_kernel(parts, paired, cut, *refs):
    total = sum(ref[...].astype(F32) for ref in refs[:parts])
    first_ref, last_ref = refs[parts:]
    first_ref[...] = total[:cut].astype(BF16)
    last_ref[...] = (merge_pairs(total[cut:]) if paired else total[cut:]).astype(last_ref.dtype)


def square_half_kernel(
    paired, chip_ref, kept_ref, arrived_ref, first_ref, first_give_ref, last_ref, last_give_ref
):
    cut = first_ref.shape[1]
    for bits in range(4):
        place = lax.bitwise_xor(chip_ref[0], bits)
        value = kept_ref[place].astype(F32) + arrived_ref[place].astype(F32)
        first, last = value[:cut], value[cut:]
        if paired:
            last = merge_pairs(last)
        low, high = bits & 1, bits >> 1
        ref = first_give_ref if low else first_ref
        ref[high] = first.astype(ref.dtype)
        ref = last_give_ref if high else last_ref
        ref[low] = last.astype(ref.dtype)


def square_next_kernel(
    paired, first_ref, first_got_ref, last_ref, last_got_ref,
    first_out_ref, first_give_ref, last_out_ref, last_give_ref,
):
    merge = merge_pairs if paired else (lambda value: value)
    first_out_ref[...] = first_ref[0] + first_got_ref[0].astype(F32)
    first_give_ref[...] = (first_ref[1] + first_got_ref[1].astype(F32)).astype(BF16)
    last_out_ref[...] = merge(last_ref[0] + last_got_ref[0].astype(F32))
    last_give_ref[...] = merge(last_ref[1] + last_got_ref[1].astype(F32)).astype(BF16)


def square_last_kernel(
    paired, first_ref, first_got_ref, last_ref, last_got_ref, first_out_ref, last_out_ref
):
    merge = merge_pairs if paired else (lambda value: value)
    first_out_ref[...] = (first_ref[...] + first_got_ref[...].astype(F32)).astype(BF16)
    last_out_ref[...] = merge(last_ref[...] + last_got_ref[...].astype(F32)).astype(last_out_ref.dtype)


def spread_pieces(core_ref, chip_ref, chips, groups, refs, store):
    step = pl.program_id(0)
    core, chip = step // chips, lax.rem(step, chips)
    apart = lax.bitwise_xor(chip, chip_ref[0])
    refs = iter(refs)
    for part, bits_lists in enumerate(groups):
        for bits_list in bits_lists:
            own_ref, other_ref = next(refs), next(refs)
            for at, bits in enumerate(bits_list):

                @pl.when((apart == bits) & (core == core_ref[0]))
                def _(part=part, ref=own_ref, at=at):
                    store(part, ref[at].astype(F32))

                @pl.when((apart == bits) & (core != core_ref[0]))
                def _(part=part, ref=other_ref, at=at):
                    store(part, ref[at].astype(F32))


def early_out_kernel(chips, groups, core_ref, chip_ref, *refs):
    gate_ref, output_ref = refs[-2:]
    out_rows, width = output_ref.shape
    channels = gate_ref.shape[1]

    def store(part, value):
        if part == 0:
            gate_ref[...] = value
        else:
            output_ref[...] = jnp.concatenate(
                [value[i * out_rows : (i + 1) * out_rows] for i in range(width // channels)], axis=1
            )

    spread_pieces(core_ref, chip_ref, chips, groups, refs[:-2], store)


def late_out_kernel(chips, groups, cut, core_ref, chip_ref, *refs):
    value_ref = refs[-1]

    def store(part, value):
        if part == 0:
            value_ref[:cut, :] = value
        else:
            value_ref[cut:, :] = value

    spread_pieces(core_ref, chip_ref, chips, groups, refs[:-1], store)


def shared_out_kernel(chips, groups, core_ref, chip_ref, *refs):
    (
        state_ref, value_kernel_ref, value_bias_ref, state_kernel_ref, state_bias_ref, skip_ref,
        gated_ref, gain_ref, own_ref, shared_ref,
    ) = refs[-10:]
    step, maps_width = state_ref.shape
    channels = own_ref.shape[1]
    lanes = channels // 128
    rows = 2 * step // lanes
    at = pl.program_id(0)

    def store(part, piece):
        stacked = jnp.concatenate(
            [piece[:rows, i * 128 : (i + 1) * 128] for i in range(lanes)], axis=0
        )
        state_ref[...] = jnp.concatenate([stacked[:step], stacked[step:]], axis=1)
        own_ref[pl.ds(at, 1), :] = piece[rows : rows + 1] + piece[rows + 1 : rows + 2]
        shared_ref[pl.ds(at, 1), :] = piece[rows + 2 : rows + 3] + piece[rows + 3 : rows + 4]

    spread_pieces(core_ref, chip_ref, chips, groups, refs[:-10], store)

    @pl.when(at == 2 * chips - 1)
    def _():
        value_kernel_ref[...] = own_ref[:KERNEL, :]
        value_bias_ref[...] = own_ref[KERNEL : KERNEL + 1, :]
        gated_ref[...] = own_ref[KERNEL + 1 : KERNEL + 2, :]
        skip_ref[...] = own_ref[KERNEL + 2 : KERNEL + 3, :]
        gain_rows = gain_ref.shape[1] // channels
        for i in range(gain_rows):
            gain_ref[:, i * channels : (i + 1) * channels] = shared_ref[i : i + 1, :]
        for i in range(0, (KERNEL + 1) * maps_width, 128):
            tap, column_to = divmod(i, maps_width)
            row, column_from = divmod(i, channels)
            value = shared_ref[gain_rows + row : gain_rows + row + 1, column_from : column_from + 128]
            if tap < KERNEL:
                state_kernel_ref[tap : tap + 1, column_to : column_to + 128] = value
            else:
                state_bias_ref[:, column_to : column_to + 128] = value


SCALAR = "scalar"
WHOLE = "whole"
BLOCKED = "blocked"
LANES = "lanes"
LEADING = "leading"
LOOSE = "loose"


def run(kernel, name, flops, args, outs, steps=None, backward=False, scratch=()):
    at = (lambda i: steps - 1 - i) if backward else (lambda i: i)

    def spec(kind, shape):
        if isinstance(kind, int):
            return pl.BlockSpec((kind,) + shape[1:], lambda i: (at(i), 0))
        if kind == SCALAR:
            return pl.BlockSpec(memory_space=pltpu.SMEM)
        if kind == LOOSE:
            return pl.BlockSpec(memory_space=pl.ANY)
        if steps is None:
            return pl.BlockSpec(memory_space=pltpu.VMEM)
        if kind == BLOCKED:
            return pl.BlockSpec((CHUNK, shape[1]), lambda i: (at(i), 0))
        if kind == LANES:
            return pl.BlockSpec((shape[0], CHUNK), lambda i: (0, at(i)))
        if kind == LEADING:
            return pl.BlockSpec((1,) + shape[1:], lambda i: (at(i),) + (0,) * (len(shape) - 1))
        return pl.BlockSpec(shape, lambda i: (0,) * len(shape))

    moved = sum(a.size * a.dtype.itemsize for kind, a in args if kind != LOOSE)
    shapes = [jax.ShapeDtypeStruct(shape, dtype) for _, shape, dtype in outs]
    moved += sum(a.size * a.dtype.itemsize for a in shapes)
    return pl.pallas_call(
        kernel,
        out_shape=shapes,
        in_specs=[spec(kind, a.shape) for kind, a in args],
        out_specs=[spec(kind, shape) for kind, shape, _ in outs],
        scratch_shapes=list(scratch),
        compiler_params=pltpu.CompilerParams(vmem_limit_bytes=VMEM_LIMIT),
        cost_estimate=pl.CostEstimate(flops=flops, bytes_accessed=moved, transcendentals=0),
        name=name,
        **({} if steps is None else {"grid": (steps,)}),
    )(*(a for _, a in args))


def per_device(
    tokens, decay_codes, norm_gain, gate_weight, value_weight, state_weight, value_kernel, value_bias,
    state_kernel, state_bias, skip_scale, gated_gain, output_weight, cotangent,
):
    tokens, decay_codes, cotangent = tokens[0], decay_codes[0], cotangent[0]
    count, own_width = tokens.shape
    heads = skip_scale.shape[0]
    channels = heads * HEAD_DIM
    head_size, chips = lax.axis_size("head"), lax.axis_size("chip")
    seq_size = 2 * chips
    width = own_width * head_size
    maps_width = 2 * NSTATE
    chunks = count // CHUNK
    core = (SCALAR, lax.axis_index("core").astype(jnp.int32)[None])
    chip = (SCALAR, lax.axis_index("chip").astype(jnp.int32)[None])
    head = (SCALAR, lax.axis_index("head").astype(jnp.int32)[None])

    parts, passed = line_parts(tokens, "head")
    before = from_behind(tokens[-HALO:], 1)
    margins = turn_all(
        jnp.concatenate([before, jnp.broadcast_to(norm_gain[None], (HALO, own_width))], axis=0),
        "head",
    )
    logs = decay_codes.astype(F32) * (-DECAY_STEP)
    input_weight = jnp.sqrt(-jnp.expm1(2.0 * logs))
    e_full, f_full, factors = run(
        decay_kernel, "decays", count * channels * 200,
        [(WHOLE, decay_codes), (WHOLE, input_weight)],
        [
            (WHOLE, (count, channels), F32),
            (WHOLE, (count, channels), F32),
            (WHOLE, (8, channels), F32),
        ],
    )
    all_logs = lax.all_to_all(
        jnp.broadcast_to(factors[None], (seq_size, 8, channels)), ("chip", "core"), 0, 0
    )[:, 7].reshape(chips, 2, channels)
    pair_logs = jnp.sum(all_logs, axis=1)
    own_logs = lax.dynamic_index_in_dim(all_logs, lax.axis_index("chip"), 0, keepdims=False)
    own_decay = jnp.exp(lax.dynamic_index_in_dim(own_logs, lax.axis_index("core"), 0))
    other_decay = jnp.exp(lax.dynamic_index_in_dim(own_logs, 1 - lax.axis_index("core"), 0))
    before_weights = decay_weights(pair_logs, False)
    after_weights = decay_weights(pair_logs, True)
    skip_full = jnp.repeat(skip_scale, HEAD_DIM)[None]

    normed, full, gain_full, scale_in, cotangent_copy = run(
        functools.partial(norm_kernel, head_size), "norm", count * width * 10,
        [head] + [(WHOLE, a) for a in [passed] + parts + margins + [cotangent]],
        [
            (WHOLE, (HALO + count, width), BF16),
            (WHOLE, (count, width), BF16),
            (WHOLE, (8, width), F32),
            (WHOLE, (count, 128), F32),
            (WHOLE, (head_size, count, own_width), BF16),
        ],
        scratch=[pltpu.VMEM((HALO, width), BF16)],
    )
    cotangent_parts = deal(cotangent_copy, "head")
    value_raw = dot(normed, value_weight).astype(BF16)
    state_raw = dot(normed, state_weight).astype(BF16)
    conv, weighted, value_slope, maps, map_slope, local_end = run(
        conv_kernel, "conv", count * channels * 400,
        [
            (WHOLE, value_raw), (WHOLE, state_raw), (WHOLE, value_kernel), (WHOLE, value_bias[None]),
            (WHOLE, state_kernel), (WHOLE, state_bias[None]), (BLOCKED, f_full), (WHOLE, factors),
        ],
        [
            (BLOCKED, (count, channels), BF16),
            (BLOCKED, (count, channels), BF16),
            (BLOCKED, (count, channels), F32),
            (BLOCKED, (count, maps_width), BF16),
            (BLOCKED, (count, maps_width), F32),
            (WHOLE, (NSTATE, channels), F32),
        ],
        steps=chunks,
    )
    state_in, _ = entering(local_end, own_decay, other_decay, before_weights, False)
    gate_pre = dot(normed[HALO:], gate_weight)
    full_cotangent = run(
        place_kernel, "place", count * width, [(WHOLE, cotangent_parts)],
        [(WHOLE, (count, width), BF16)],
    )[0]
    mixed_grad = dot_nt(full_cotangent, output_weight)
    mixer, stats, high, low = run(
        mixer_kernel, "mixer", count * channels * 1000,
        [
            (WHOLE, state_in), (BLOCKED, maps), (BLOCKED, weighted), (BLOCKED, conv),
            (BLOCKED, e_full), (WHOLE, factors), (WHOLE, skip_full), (BLOCKED, gate_pre),
            (BLOCKED, mixed_grad), (WHOLE, gated_gain[None]),
        ],
        [
            (BLOCKED, (count, channels), F32),
            (LANES, (8, count), F32),
            (LEADING, (chunks, NSTATE, channels), BF16),
            (LEADING, (chunks, NSTATE, channels), BF16),
        ],
        steps=chunks,
        scratch=[pltpu.VMEM((NSTATE, channels), F32)],
    )
    mixed, gate_grad, mixer_grad, gate_small, start_grad = run(
        functools.partial(gate_kernel, float(channels * head_size), chunks, head_size),
        "gate", count * channels * 600,
        [(LANES, part) for part in turn_all(stats, "head")]
        + [
            (BLOCKED, mixer), (BLOCKED, gate_pre), (BLOCKED, mixed_grad), (WHOLE, gated_gain[None]),
            (BLOCKED, conv), (BLOCKED, e_full), (WHOLE, factors), (BLOCKED, maps),
        ],
        [
            (BLOCKED, (count, channels), BF16),
            (BLOCKED, (count, channels), BF16),
            (BLOCKED, (count, channels), F32),
            (WHOLE, (8, channels), F32),
            (WHOLE, (NSTATE, channels), F32),
        ],
        steps=chunks,
        backward=True,
    )
    grad_after, pair = entering(start_grad, own_decay, other_decay, after_weights, True)

    out_parts = run(
        out_kernel, "out", 2 * count * channels * width,
        [(LOOSE, start_grad), (WHOLE, mixed), (WHOLE, output_weight)],
        [(WHOLE, (head_size, count, own_width), BF16)],
    )[0]
    step, out_rows = width // seq_size, channels // seq_size
    rows = step + out_rows * (width // channels)
    early_kept, early_given, early_gain = run(
        early_kernel, "early", 4 * count * channels * width,
        [
            (LOOSE, pair), core, (WHOLE, normed), (WHOLE, gate_grad), (WHOLE, mixed),
            (WHOLE, full_cotangent), (WHOLE, gate_weight),
        ],
        [(WHOLE, (chips, rows, channels), BF16)] * 2 + [(WHOLE, (1, width), F32)],
        scratch=[pltpu.VMEM((channels, width), F32)],
    )
    early_gate, early_out, early_mark = sum_pieces(
        chip, early_kept, early_given, step, False, "early"
    )
    branch = jnp.sum(deal(out_parts, "head").astype(F32), axis=0)
    block_out = (tokens.astype(F32) + branch).astype(BF16)

    value_grads, map_grads = run(
        functools.partial(back_kernel, chunks), "back", count * channels * 2000,
        [
            (LOOSE, early_given), (LOOSE, out_parts), (WHOLE, grad_after), (BLOCKED, mixer_grad), (BLOCKED, e_full),
            (BLOCKED, f_full), (WHOLE, factors), (BLOCKED, weighted), (LEADING, high),
            (LEADING, low), (BLOCKED, maps), (BLOCKED, value_slope), (BLOCKED, map_slope),
            (WHOLE, skip_full),
        ],
        [(BLOCKED, (count, channels), F32), (BLOCKED, (count, maps_width), F32)],
        steps=chunks,
        backward=True,
        scratch=[pltpu.VMEM((NSTATE, channels), F32)],
    )
    after = from_behind(jnp.concatenate([value_grads[:8], map_grads[:8]], axis=1), -1)
    value_raw_grad, state_raw_grad, value_small, state_small = run(
        functools.partial(conv_back_kernel, chunks), "conv_back", count * channels * 100,
        [
            (LOOSE, early_mark), (BLOCKED, value_grads), (BLOCKED, map_grads), (WHOLE, after),
            (WHOLE, value_raw), (WHOLE, state_raw), (WHOLE, value_kernel), (WHOLE, state_kernel),
        ],
        [
            (BLOCKED, (count, channels), BF16),
            (BLOCKED, (count, maps_width), BF16),
            (WHOLE, (8, channels), F32),
            (WHOLE, (8, maps_width), F32),
        ],
        steps=chunks,
        backward=True,
        scratch=[pltpu.VMEM((8, channels), F32), pltpu.VMEM((8, maps_width), F32)],
    )
    lanes = channels // 128
    state_rows = 2 * step // lanes
    late_rows = step + state_rows + HALO
    late_kept, late_given = run(
        late_kernel, "late", 3 * count * channels * width,
        [
            core, (WHOLE, normed), (WHOLE, value_raw_grad), (WHOLE, state_raw_grad),
            (WHOLE, value_small), (WHOLE, gate_small), (WHOLE, early_gain), (WHOLE, state_small),
            (WHOLE, value_weight), (WHOLE, state_weight), (WHOLE, gain_full),
        ],
        [(WHOLE, (chips, late_rows, channels), BF16)] * 2,
        scratch=[
            pltpu.VMEM((HALO, channels), F32),
            pltpu.VMEM((HALO, channels), F32),
            pltpu.VMEM((8, width), F32),
            pltpu.VMEM((width, channels + maps_width), F32),
        ],
    )
    normed_parts = run(
        normed_kernel, "normed", 4 * count * channels * width,
        [
            (LOOSE, late_given), (WHOLE, gate_grad), (WHOLE, value_raw_grad),
            (WHOLE, state_raw_grad), (WHOLE, gate_weight), (WHOLE, value_weight),
            (WHOLE, state_weight), (WHOLE, full), (WHOLE, gain_full),
        ],
        [(WHOLE, (head_size, count + HALO, own_width), BF16)],
    )[0]
    normed_parts = deal(normed_parts, "head")
    late_cut = step // 3 * 2 // 16 * 16
    late_first, late_rest, _ = sum_pieces(chip, late_kept, late_given, late_cut, True, "late")
    late_last, shared_piece = late_rest[: step - late_cut].astype(BF16), late_rest[step - late_cut :]
    summed = butterfly(shared_piece, "head")
    line = jnp.arange(late_rows - step)[:, None]
    own_line = (line >= state_rows) & (line < state_rows + 2)
    tail = summed[state_rows + 2 : state_rows + 3] + summed[state_rows + 3 : state_rows + 4]
    tail_high = tail.astype(BF16).astype(F32)
    summed = jnp.where(
        line == state_rows + 2, tail_high, jnp.where(line == state_rows + 3, tail - tail_high, summed)
    )
    shared_piece = jnp.where(own_line, shared_piece, summed).astype(BF16)

    def unpack(kernel, name, pieces, outs, flops, extra=(), scratch=()):
        groups = [collect(piece, order) for piece, order in pieces]
        bits = [[found[2] for found in group] for group in groups]
        arrays = [(WHOLE, value) for group in groups for found in group for value in found[:2]]
        return run(
            functools.partial(kernel, chips, bits, *extra), name, flops, [core, chip] + arrays, outs,
            steps=seq_size, scratch=scratch,
        )

    gate_weight_gradient, output_weight_gradient = unpack(
        early_out_kernel, "early_out", [(early_gate, (2, 1)), (early_out, (1, 2))],
        [(step, (width, channels), F32), (out_rows, (channels, width), F32)], 4 * channels * width,
    )
    value_weight_gradient = unpack(
        late_out_kernel, "late_out", [(late_first, (2, 1)), (late_last, (1, 2))],
        [(step, (width, channels), F32)], 2 * channels * width, extra=(late_cut,),
    )[0]
    (
        state_weight_gradient, value_kernel_gradient, value_bias_gradient, state_kernel_gradient,
        state_bias_gradient, skip_sums, gated_gain_gradient, gain_sums,
    ) = unpack(
        shared_out_kernel, "shared_out", [(shared_piece, (2, 1))],
        [
            (step, (width, maps_width), F32),
            (WHOLE, (KERNEL, channels), F32),
            (WHOLE, (1, channels), F32),
            (WHOLE, (KERNEL, maps_width), F32),
            (WHOLE, (1, maps_width), F32),
            (WHOLE, (1, channels), F32),
            (WHOLE, (1, channels), F32),
            (WHOLE, (1, width), F32),
        ],
        2 * maps_width * width,
        scratch=[pltpu.VMEM((HALO, channels), F32), pltpu.VMEM((HALO, channels), F32)],
    )
    value_bias_gradient, state_bias_gradient = value_bias_gradient[0], state_bias_gradient[0]
    gated_gain_gradient = gated_gain_gradient[0]
    skip_scale_gradient = jnp.sum(skip_sums.reshape(heads, HEAD_DIM), axis=1)
    norm_gain_gradient = lax.dynamic_slice_in_dim(
        gain_sums[0], lax.axis_index("head") * own_width, own_width, 0
    )

    tokens_gradient = run(
        functools.partial(last_kernel, float(width)), "last", count * own_width * 20,
        [
            (LOOSE, gate_weight_gradient), (WHOLE, normed_parts), (WHOLE, tokens), (WHOLE, scale_in),
            (WHOLE, norm_gain[None]), (WHOLE, cotangent),
        ],
        [(WHOLE, (count, own_width), BF16)],
    )[0]
    return (
        block_out[None],
        tokens_gradient[None],
        norm_gain_gradient,
        gate_weight_gradient,
        value_weight_gradient,
        state_weight_gradient,
        value_kernel_gradient,
        value_bias_gradient,
        state_kernel_gradient,
        state_bias_gradient,
        skip_scale_gradient,
        gated_gain_gradient,
        output_weight_gradient,
    )


def solution(mesh):
    seq_size, head_size = mesh.shape["seq"], mesh.shape["head"]
    mesh = Mesh(mesh.devices.reshape(seq_size // 2, 2, head_size), ("chip", "core", "head"))
    seq = ("chip", "core")
    in_specs = (
        P(None, seq, "head"),
        P(None, seq, "head"),
        P("head"),
        P(None, "head"),
        P(None, "head"),
        P(),
        P(None, "head"),
        P("head"),
        P(),
        P(),
        P("head"),
        P("head"),
        P("head", None),
        P(None, seq, "head"),
    )
    out_specs = (
        P(None, seq, "head"),
        P(None, seq, "head"),
        P("head"),
        P(None, "head"),
        P(None, "head"),
        P(),
        P(None, "head"),
        P("head"),
        P(),
        P(),
        P("head"),
        P("head"),
        P("head", None),
    )
    return jax.shard_map(
        per_device, mesh=mesh, in_specs=in_specs, out_specs=out_specs, check_vma=False
    )
```

profile of v0, /device:TPU:1, one launch (start us, length us, event | category | flops | bytes accessed | tf_op | source)
XLA Modules:
  0.0 310.9 jit_solution(17902982287111387194)
XLA Ops:
  0.7 3.2 %collective-permute-start = (bf16[512,384]{1,0:T(8,128)(2,1)}, bf16[512,384]{1,0:T(8,128)(2,1)S(1)}, u32[]{:S(2)}, u32[]{:S(2)}) collective-permute-start(bf16[512,384]{1,0:T(8,128)(2,1)} %bitcast.33), channel_id=1, source_target_pairs={{0,2},{1,3},{2,0},{3,1},{4,6},{5,7},{6,4},{7,5},{8,10},{9,11},{10,... | collective-permute-start | bytes 1179656 | tf_op jit(solution)/shard_map/ppermute | solution.py:39
  3.9 3.2 %collective-permute-start.2 = (bf16[512,384]{1,0:T(8,128)(2,1)}, bf16[512,384]{1,0:T(8,128)(2,1)S(1)}, u32[]{:S(2)}, u32[]{:S(2)}) collective-permute-start(bf16[512,384]{1,0:T(8,128)(2,1)} %bitcast.34), channel_id=1, source_target_pairs={{0,1},{1,2},{2,3},{4,5},{5,6},{6,7},{8,9},{9,10},{10,11},{12,13},{... | collective-permute-start | bytes 1179656 | tf_op jit(solution)/shard_map/ppermute | solution.py:50
  9.1 4.2 %collective-permute-start.4 = (bf16[16,384]{1,0:T(8,128)(2,1)S(1)}, bf16[16,384]{1,0:T(8,128)(2,1)S(1)}, u32[]{:S(2)}, u32[]{:S(2)}) collective-permute-start(bf16[16,384]{1,0:T(8,128)(2,1)S(1)} %slice_bitcast_fusion), channel_id=1, source_target_pairs={{0,4},{4,8},{8,12},{12,16},{16,20},{20,24},{24,28},{1,5},{5,9},{9,... | collective-permute-start | bytes 36872 | tf_op jit(solution)/shard_map/ppermute | solution.py:30
  14.2 7.2 %collective-permute-done.refs_2_ = bf16[512,384]{1,0:T(8,128)(2,1)S(1)} collective-permute-done((bf16[512,384]{1,0:T(8,128)(2,1)}, bf16[512,384]{1,0:T(8,128)(2,1)S(1)}, u32[]{:S(2)}, u32[]{:S(2)}) %collective-permute-start) | collective-permute-done | bytes 393248 | tf_op jit(solution)/shard_map/ppermute | solution.py:39
  27.3 6.1 %all-to-all-start = ((f32[8,8,768]{2,1,0:T(8,128)}), f32[8,8,768]{2,1,0:T(8,128)S(1)}, u32[]{:S(2)}, u32[]{:S(2)}) async-start(f32[8,8,768]{2,1,0:T(8,128)} %broadcast_in_dim.135), calls=%async_computation | async-start | bytes 393216 | tf_op jit(solution)/shard_map/all_to_all | solution.py:876
  33.5 3.2 %collective-permute-start.5 = (bf16[32,384]{1,0:T(8,128)(2,1)S(1)}, bf16[32,384]{1,0:T(8,128)(2,1)S(1)}, u32[]{:S(2)}, u32[]{:S(2)}) collective-permute-start(bf16[32,384]{1,0:T(8,128)(2,1)S(1)} %pad_maximum_fusion.6.refs_4_), channel_id=1, source_target_pairs={{0,1},{1,2},{2,3},{3,0},{4,5},{5,6},{6,7},{7,4},{8,9},{9,10},{10,1... | collective-permute-start | bytes 73736 | tf_op jit(solution)/shard_map/ppermute | solution.py:39
  51.8 4.6 %all-to-all-start.1 = ((bf16[4,512,384]{2,1,0:T(8,128)(2,1)}), bf16[4,512,384]{2,1,0:T(8,128)(2,1)S(1)}, u32[]{:S(2)}, u32[]{:S(2)}) async-start(bf16[4,512,384]{2,1,0:T(8,128)(2,1)} %copy-done.27), calls=%async_computation.1 | async-start | bytes 3145728 | tf_op jit(solution)/shard_map/all_to_all | solution.py:57
  58.9 4.5 %conv.1 = (bf16[512,768]{1,0:T(8,128)(2,1)S(1)}, bf16[512,768]{1,0:T(8,128)(2,1)S(1)}, f32[512,768]{1,0:T(8,128)S(1)}, bf16[512,256]{1,0:T(8,128)(2,1)S(1)}, f32[512,256]{1,0:T(8,128)S(1)}, /*index=5*/f32[128,768]{1,0:T(8,128)}) custom-call(bf16[528,768]{1,0:T(8,128)(2,1)S(1)} %copy-done.6, ...), custom_call_target="tpu_custom_call" | custom-call | flops 157286400 | bytes 7014400 | tf_op jit(solution)/shard_map/conv/pallas_call | solution.py:829
  85.2 7.5 %collective-permute-done.10 = f32[64,768]{1,0:T(8,128)S(1)} collective-permute-done((f32[64,768]{1,0:T(8,128)S(1)}, f32[64,768]{1,0:T(8,128)S(1)}, u32[]{:S(2)}, u32[]{:S(2)}) %collective-permute-start.10) | collective-permute-done | bytes 196640 | tf_op jit(solution)/shard_map/ppermute | solution.py:61
  94.8 4.7 %fusion.gate_ref.refs_5_ = f32[512,768]{1,0:T(8,128)} fusion(bf16[1536,768]{1,0:T(8,128)(2,1)} %gate_weight_ref.1, bf16[528,1536]{1,0:T(8,128)(2,1)} %copy-done.68), kind=kOutput, calls=%fused_computation.1 | convolution fusion | flops 1207959552 | bytes 5505024 | tf_op jit(solution)/shard_map/dot_general | solution.py:173
  115.3 3.2 %gate.1 = (bf16[512,768]{1,0:T(8,128)(2,1)S(1)}, bf16[512,768]{1,0:T(8,128)(2,1)S(1)}, f32[512,768]{1,0:T(8,128)S(1)}, f32[8,768]{1,0:T(8,128)S(1)}, f32[128,768]{1,0:T(8,128)S(1)}) custom-call(f32[8,512]{1,0:T(8,128)S(1)} %get-tuple-element.86.refs_0_, f32[8,512]{1,0:T(8,128)S(1)} %collective-permute-done.13.refs_1_, ...), custom_call_target="tpu_custom_call" | custom-call | flops 235929600 | bytes 10995200 | tf_op jit(solution)/shard_map/gate/pallas_call | solution.py:829
  123.5 6.1 %early.1 = (bf16[4,384,768]{2,1,0:T(8,128)(2,1)S(1)}, bf16[4,384,768]{2,1,0:T(8,128)(2,1)}, f32[1,1536]{1,0:T(1,128)S(1)}) custom-call(f32[64,768]{1,0:T(8,128)S(1)} %add_select_fusion.2.pair_ref, s32[1]{0:T(128)} %bitcast.6.core_ref, bf16[528,1536]{1,0:T(8,128)(2,1)S(1)} %copy-done.69, bf16[512,768]{1,0:T(8,128)(2,1)S(1)} %get-tuple-element.90.gate_ref.gate_grad_ref, ...), custom_call_target="tpu_custom_call" | custom-call | flops 2415919104 | bytes 11851780 | tf_op jit(solution)/shard_map/early/pallas_call | solution.py:829
  134.2 3.6 %collective-permute-done.30 = f32[64,768]{1,0:T(8,128)S(1)} collective-permute-done((f32[64,768]{1,0:T(8,128)S(1)}, f32[64,768]{1,0:T(8,128)S(1)}, u32[]{:S(2)}, u32[]{:S(2)}) %collective-permute-start.30) | collective-permute-done | bytes 196640 | tf_op jit(solution)/shard_map/ppermute | solution.py:61
  137.8 4.1 %collective-permute-done.31 = f32[64,768]{1,0:T(8,128)S(1)} collective-permute-done((f32[64,768]{1,0:T(8,128)S(1)}, f32[64,768]{1,0:T(8,128)S(1)}, u32[]{:S(2)}, u32[]{:S(2)}) %collective-permute-start.31) | collective-permute-done | bytes 196640 | tf_op jit(solution)/shard_map/ppermute | solution.py:61
  145.1 3.0 out.1.out_ref
  148.0 4.5 %all-to-all-start.2 = ((bf16[4,512,384]{2,1,0:T(8,128)(2,1)}), bf16[4,512,384]{2,1,0:T(8,128)(2,1)}, u32[]{:S(2)}, u32[]{:S(2)}) async-start(bf16[4,512,384]{2,1,0:T(8,128)(2,1)} %out.1.out_ref), calls=%async_computation.2 | async-start | bytes 3145728 | tf_op jit(solution)/shard_map/all_to_all | solution.py:57
  161.8 5.1 %back.1 = (f32[512,768]{1,0:T(8,128)S(1)}, f32[512,256]{1,0:T(8,128)S(1)}) custom-call(bf16[4,384,768]{2,1,0:T(8,128)(2,1)} %get-tuple-element.92.early_ref, bf16[4,512,384]{2,1,0:T(8,128)(2,1)} %out.1.out_ref, f32[128,768]{1,0:T(8,128)S(1)} %add_select_fusion.state_in_ref, f32[512,768]{1,0:T(8,128)S(1)} %copy-done.32, ...), custom_call_target="tpu_custom_call" | custom-call | flops 786432000 | bytes 11955200 | tf_op jit(solution)/shard_map/back/pallas_call | solution.py:829
  172.4 3.1 %conv_back.1 = (bf16[512,768]{1,0:T(8,128)(2,1)S(1)}, bf16[512,256]{1,0:T(8,128)(2,1)S(1)}, f32[8,768]{1,0:T(8,128)S(1)}, f32[8,256]{1,0:T(8,128)S(1)}) custom-call(f32[2,192,768]{2,1,0:T(8,128)S(1)} %get-tuple-element.93.first_ref.other_ref, f32[512,768]{1,0:T(8,128)S(1)} %get-tuple-element.109.value_ref, f32[512,256]{1,0:T(8,128)S(1)} %get-tuple-element.110.map_ref, ...), custom_call_target="tpu_custom_call" | custom-call | flops 39321600 | bytes 4300800 | tf_op jit(solution)/shard_map/conv_back/pallas_call | solution.py:829
  175.6 3.1 late.1
  180.7 12.9 %collective-permute-done.18.first_got_ref = bf16[2,192,768]{2,1,0:T(8,128)(2,1)S(1)} collective-permute-done((bf16[2,192,768]{2,1,0:T(8,128)(2,1)S(1)}, bf16[2,192,768]{2,1,0:T(8,128)(2,1)S(1)}, u32[]{:S(2)}, u32[]{:S(2)}) %collective-permute-start.18) | collective-permute-done | bytes 589856 | tf_op jit(solution)/shard_map/ppermute | solution.py:61
  204.4 5.3 %normed.1 = bf16[4,528,384]{2,1,0:T(8,128)(2,1)} custom-call(bf16[4,272,768]{2,1,0:T(8,128)(2,1)S(1)} %get-tuple-element.118.late_ref, bf16[512,768]{1,0:T(8,128)(2,1)S(1)} %copy-done.37, bf16[512,768]{1,0:T(8,128)(2,1)S(1)} %get-tuple-element.111.value_ref.value_grad_ref, bf16[512,256]{1,0:T(8,128)(2,1)S(1)} %get-tuple-element.112.state_ref.state_grad_ref, ...), custom_call_target="tpu_custom_call" | custom-call | flops 2415919104 | bytes 10584064 | tf_op jit(solution)/shard_map/normed/pallas_call | solution.py:829
  209.7 4.8 %all-to-all-start.3 = ((bf16[4,528,384]{2,1,0:T(8,128)(2,1)}), bf16[4,528,384]{2,1,0:T(8,128)(2,1)S(1)}, u32[]{:S(2)}, u32[]{:S(2)}) async-start(bf16[4,528,384]{2,1,0:T(8,128)(2,1)} %normed.1), calls=%async_computation.3 | async-start | bytes 3244032 | tf_op jit(solution)/shard_map/all_to_all | solution.py:57
  225.6 11.7 %collective-permute-start.27 = (bf16[2,192,768]{2,1,0:T(8,128)(2,1)S(1)}, bf16[2,192,768]{2,1,0:T(8,128)(2,1)S(1)}, u32[]{:S(2)}, u32[]{:S(2)}) collective-permute-start(bf16[2,192,768]{2,1,0:T(8,128)(2,1)S(1)} %pad_maximum_fusion.1.refs_4_), channel_id=1, source_target_pairs={{0,4},{4,0},{1,5},{5,1},{2,6},{6,2},{3,7},{7,3},{8,12},{12,8},{9,1... | collective-permute-start | bytes 1769480 | tf_op jit(solution)/shard_map/ppermute | solution.py:34
  238.5 2.8 collective-permute-done.40
  241.3 4.3 %collective-permute-start.41 = (f32[80,768]{1,0:T(8,128)S(1)}, f32[80,768]{1,0:T(8,128)S(1)}, u32[]{:S(2)}, u32[]{:S(2)}) collective-permute-start(f32[80,768]{1,0:T(8,128)S(1)} %slice_add_fusion.1), channel_id=1, source_target_pairs={{0,2},{1,3},{2,0},{3,1},{4,6},{5,7},{6,4},{7,5},{8,10},{9,11},{10,... | collective-permute-start | bytes 737288 | tf_op jit(solution)/shard_map/ppermute | solution.py:72
  245.6 8.9 %collective-permute-start.23 = (bf16[2,192,768]{2,1,0:T(8,128)(2,1)S(1)}, bf16[2,192,768]{2,1,0:T(8,128)(2,1)S(1)}, u32[]{:S(2)}, u32[]{:S(2)}) collective-permute-start(bf16[2,192,768]{2,1,0:T(8,128)(2,1)S(1)} %pad_maximum_fusion.refs_0_), channel_id=1, source_target_pairs={{0,4},{4,0},{1,5},{5,1},{2,6},{6,2},{3,7},{7,3},{8,12},{12,8},{9,1... | collective-permute-start | bytes 1769480 | tf_op jit(solution)/shard_map/ppermute | solution.py:34
  255.9 6.5 %collective-permute-done.41 = f32[80,768]{1,0:T(8,128)S(1)} collective-permute-done((f32[80,768]{1,0:T(8,128)S(1)}, f32[80,768]{1,0:T(8,128)S(1)}, u32[]{:S(2)}, u32[]{:S(2)}) %collective-permute-start.41) | collective-permute-done | bytes 245792 | tf_op jit(solution)/shard_map/ppermute | solution.py:72
  263.7 4.1 %collective-permute-done.42 = bf16[80,768]{1,0:T(8,128)(2,1)S(1)} collective-permute-done((bf16[80,768]{1,0:T(8,128)(2,1)S(1)}, bf16[80,768]{1,0:T(8,128)(2,1)S(1)}, u32[]{:S(2)}, u32[]{:S(2)}) %collective-permute-start.42) | collective-permute-done | bytes 122912 | tf_op jit(solution)/shard_map/ppermute | solution.py:61
  267.8 5.8 %collective-permute-done.50 = bf16[64,768]{1,0:T(8,128)(2,1)S(1)} collective-permute-done((bf16[64,768]{1,0:T(8,128)(2,1)S(1)}, bf16[64,768]{1,0:T(8,128)(2,1)S(1)}, u32[]{:S(2)}, u32[]{:S(2)}) %collective-permute-start.50) | collective-permute-done | bytes 98336 | tf_op jit(solution)/shard_map/ppermute | solution.py:61
  286.4 6.4 %early_out.1 = (f32[1536,768]{1,0:T(8,128)}, f32[768,1536]{1,0:T(8,128)}) custom-call(s32[1]{0:T(128)} %bitcast.6.core_ref, s32[1]{0:T(128)} %bitcast.7.chip_ref, bf16[2,192,768]{2,1,0:T(8,128)(2,1)S(1)} %pad_maximum_fusion.refs_0_, bf16[2,192,768]{2,1,0:T(8,128)(2,1)S(1)} %copy-done.53, bf16[2,192,768]{2,1,0:T(8,128)(2,1)} %collective-permute-done.24.refs_2_, ...), custom_call_target="tpu_custom_call" | custom-call | flops 4718592 | bytes 14155784 | tf_op jit(solution)/shard_map/early_out/pallas_call | solution.py:829
  298.3 5.7 %late_out.1 = f32[1536,768]{1,0:T(8,128)} custom-call(s32[1]{0:T(128)} %bitcast.6.core_ref, s32[1]{0:T(128)} %bitcast.7.chip_ref, bf16[2,128,768]{2,1,0:T(8,128)(2,1)} %pad_maximum_fusion.2.refs_0_, bf16[2,128,768]{2,1,0:T(8,128)(2,1)} %collective-permute-done.47.refs_1_, bf16[2,128,768]{2,1,0:T(8,128)(2,1)} %collective-permute-done.48.refs_2_, ...), custom_call_target="tpu_custom_call" | custom-call | flops 2359296 | bytes 7077896 | tf_op jit(solution)/shard_map/late_out/pallas_call | solution.py:829
  304.0 4.3 %shared_out.1 = (f32[1536,256]{1,0:T(8,128)}, f32[4,768]{1,0:T(4,128)}, f32[1,768]{1,0:T(1,128)S(1)}, f32[4,256]{1,0:T(4,128)}, f32[1,256]{1,0:T(1,128)}, /*inde...) custom-call(s32[1]{0:T(128)} %bitcast.6.core_ref, s32[1]{0:T(128)} %bitcast.7.chip_ref, ...), custom_call_target="tpu_custom_call" | custom-call | flops 786432 | bytes 2588680 | tf_op jit(solution)/shard_map/shared_out/pallas_call | solution.py:829
  (348 shorter events, 141.7 us)
Async XLA Ops:
  0.7 20.7 %collective-permute-start = (bf16[512,384]{1,0:T(8,128)(2,1)}, bf16[512,384]{1,0:T(8,128)(2,1)S(1)}, u32[]{:S(2)}, u32[]{:S(2)}) collective-permute-start(bf16[512,384]{1,0:T(8,128)(2,1)} %bitcast.33), channel_id=1, source_target_pairs={{0,2},{1,3},{2,0},{3,1},{4,6},{5,7},{6,4},{7,5},{8,10},{9,11},{10,... | collective-permute-start | bytes 1179656 | tf_op jit(solution)/shard_map/ppermute | solution.py:39
  3.9 37.7 %collective-permute-start.2 = (bf16[512,384]{1,0:T(8,128)(2,1)}, bf16[512,384]{1,0:T(8,128)(2,1)S(1)}, u32[]{:S(2)}, u32[]{:S(2)}) collective-permute-start(bf16[512,384]{1,0:T(8,128)(2,1)} %bitcast.34), channel_id=1, source_target_pairs={{0,1},{1,2},{2,3},{4,5},{5,6},{6,7},{8,9},{9,10},{10,11},{12,13},{... | collective-permute-start | bytes 1179656 | tf_op jit(solution)/shard_map/ppermute | solution.py:50
  7.1 34.5 %collective-permute-start.3 = (bf16[512,384]{1,0:T(8,128)(2,1)}, bf16[512,384]{1,0:T(8,128)(2,1)}, u32[]{:S(2)}, u32[]{:S(2)}) collective-permute-start(bf16[512,384]{1,0:T(8,128)(2,1)} %bitcast.35), channel_id=1, source_target_pairs={{1,0},{2,1},{3,2},{5,4},{6,5},{7,6},{9,8},{10,9},{11,10},{13,12},{... | collective-permute-start | bytes 1179656 | tf_op jit(solution)/shard_map/ppermute | solution.py:51
  9.1 24.3 %collective-permute-start.4 = (bf16[16,384]{1,0:T(8,128)(2,1)S(1)}, bf16[16,384]{1,0:T(8,128)(2,1)S(1)}, u32[]{:S(2)}, u32[]{:S(2)}) collective-permute-start(bf16[16,384]{1,0:T(8,128)(2,1)S(1)} %slice_bitcast_fusion), channel_id=1, source_target_pairs={{0,4},{4,8},{8,12},{12,16},{16,20},{20,24},{24,28},{1,5},{5,9},{9,... | collective-permute-start | bytes 36872 | tf_op jit(solution)/shard_map/ppermute | solution.py:30
  21.4 20.2 %collective-permute-start.1 = (bf16[512,384]{1,0:T(8,128)(2,1)S(1)}, bf16[512,384]{1,0:T(8,128)(2,1)}, u32[]{:S(2)}, u32[]{:S(2)}) collective-permute-start(bf16[512,384]{1,0:T(8,128)(2,1)S(1)} %collective-permute-done.refs_2_), channel_id=1, source_target_pairs={{2,3},{1,0},{6,7},{5,4},{10,11},{9,8},{14,15},{13,12},{18,19},{17,... | collective-permute-start | bytes 1179656 | tf_op jit(solution)/shard_map/ppermute | solution.py:52
  27.3 23.8 %all-to-all-start = ((f32[8,8,768]{2,1,0:T(8,128)}), f32[8,8,768]{2,1,0:T(8,128)S(1)}, u32[]{:S(2)}, u32[]{:S(2)}) async-start(f32[8,8,768]{2,1,0:T(8,128)} %broadcast_in_dim.135), calls=%async_computation | async-start | bytes 393216 | tf_op jit(solution)/shard_map/all_to_all | solution.py:876
  51.8 49.5 %all-to-all-start.1 = ((bf16[4,512,384]{2,1,0:T(8,128)(2,1)}), bf16[4,512,384]{2,1,0:T(8,128)(2,1)S(1)}, u32[]{:S(2)}, u32[]{:S(2)}) async-start(bf16[4,512,384]{2,1,0:T(8,128)(2,1)} %copy-done.27), calls=%async_computation.1 | async-start | bytes 3145728 | tf_op jit(solution)/shard_map/all_to_all | solution.py:57
  67.9 12.5 %collective-permute-start.8 = (f32[128,768]{1,0:T(8,128)}, f32[128,768]{1,0:T(8,128)}, u32[]{:S(2)}, u32[]{:S(2)}) collective-permute-start(f32[128,768]{1,0:T(8,128)} %get-tuple-element.80), channel_id=1, source_target_pairs={{0,4},{4,0},{1,5},{5,1},{2,6},{6,2},{3,7},{7,3},{8,12},{12,8},{9,1... | collective-permute-start | bytes 1179656 | tf_op jit(solution)/shard_map/ppermute | solution.py:34
  131.0 38.0 %collective-permute-start.17 = (bf16[4,384,768]{2,1,0:T(8,128)(2,1)}, bf16[4,384,768]{2,1,0:T(8,128)(2,1)}, u32[]{:S(2)}, u32[]{:S(2)}) collective-permute-start(bf16[4,384,768]{2,1,0:T(8,128)(2,1)} %get-tuple-element.92.early_ref), channel_id=1, source_target_pairs={{0,4},{4,0},{1,5},{5,1},{2,6},{6,2},{3,7},{7,3},{8,12},{12,8},{9,1... | collective-permute-start | bytes 7077896 | tf_op jit(solution)/shard_map/ppermute | solution.py:34
  148.0 61.7 %all-to-all-start.2 = ((bf16[4,512,384]{2,1,0:T(8,128)(2,1)}), bf16[4,512,384]{2,1,0:T(8,128)(2,1)}, u32[]{:S(2)}, u32[]{:S(2)}) async-start(bf16[4,512,384]{2,1,0:T(8,128)(2,1)} %out.1.out_ref), calls=%async_computation.2 | async-start | bytes 3145728 | tf_op jit(solution)/shard_map/all_to_all | solution.py:57
  178.7 17.5 %collective-permute-start.35 = (bf16[4,272,768]{2,1,0:T(8,128)(2,1)S(1)}, bf16[4,272,768]{2,1,0:T(8,128)(2,1)S(1)}, u32[]{:S(2)}, u32[]{:S(2)}) collective-permute-start(bf16[4,272,768]{2,1,0:T(8,128)(2,1)S(1)} %get-tuple-element.118.late_ref), channel_id=1, source_target_pairs={{0,4},{4,0},{1,5},{5,1},{2,6},{6,2},{3,7},{7,3},{8,12},{12,8},{9,1... | collective-permute-start | bytes 5013512 | tf_op jit(solution)/shard_map/ppermute | solution.py:34
  178.7 14.9 %collective-permute-start.18 = (bf16[2,192,768]{2,1,0:T(8,128)(2,1)S(1)}, bf16[2,192,768]{2,1,0:T(8,128)(2,1)S(1)}, u32[]{:S(2)}, u32[]{:S(2)}) collective-permute-start(bf16[2,192,768]{2,1,0:T(8,128)(2,1)S(1)} %get-tuple-element.94), channel_id=1, source_target_pairs={{0,8},{8,0},{16,24},{24,16},{1,9},{9,1},{17,25},{25,17},{2,10},{10... | collective-permute-start | bytes 1769480 | tf_op jit(solution)/shard_map/ppermute | solution.py:61
  180.4 14.2 %collective-permute-start.19 = (bf16[2,192,768]{2,1,0:T(8,128)(2,1)S(1)}, bf16[2,192,768]{2,1,0:T(8,128)(2,1)S(1)}, u32[]{:S(2)}, u32[]{:S(2)}) collective-permute-start(bf16[2,192,768]{2,1,0:T(8,128)(2,1)S(1)} %get-tuple-element.96), channel_id=1, source_target_pairs={{0,16},{8,24},{16,0},{24,8},{1,17},{9,25},{17,1},{25,9},{2,18},{10... | collective-permute-start | bytes 1769480 | tf_op jit(solution)/shard_map/ppermute | solution.py:61
  198.0 17.1 %collective-permute-start.37 = (bf16[2,144,768]{2,1,0:T(8,128)(2,1)}, bf16[2,144,768]{2,1,0:T(8,128)(2,1)S(1)}, u32[]{:S(2)}, u32[]{:S(2)}) collective-permute-start(bf16[2,144,768]{2,1,0:T(8,128)(2,1)} %get-tuple-element.125), channel_id=1, source_target_pairs={{0,16},{8,24},{16,0},{24,8},{1,17},{9,25},{17,1},{25,9},{2,18},{10... | collective-permute-start | bytes 1327112 | tf_op jit(solution)/shard_map/ppermute | solution.py:61
  198.6 16.6 %collective-permute-start.36 = (bf16[2,128,768]{2,1,0:T(8,128)(2,1)}, bf16[2,128,768]{2,1,0:T(8,128)(2,1)}, u32[]{:S(2)}, u32[]{:S(2)}) collective-permute-start(bf16[2,128,768]{2,1,0:T(8,128)(2,1)} %get-tuple-element.123), channel_id=1, source_target_pairs={{0,8},{8,0},{16,24},{24,16},{1,9},{9,1},{17,25},{25,17},{2,10},{10... | collective-permute-start | bytes 1179656 | tf_op jit(solution)/shard_map/ppermute | solution.py:61
  204.1 15.1 %collective-permute-start.26 = (bf16[192,768]{1,0:T(8,128)(2,1)}, bf16[192,768]{1,0:T(8,128)(2,1)}, u32[]{:S(2)}, u32[]{:S(2)}) collective-permute-start(bf16[192,768]{1,0:T(8,128)(2,1)} %get-tuple-element.102), channel_id=1, source_target_pairs={{0,8},{8,0},{16,24},{24,16},{1,9},{9,1},{17,25},{25,17},{2,10},{10... | collective-permute-start | bytes 884744 | tf_op jit(solution)/shard_map/ppermute | solution.py:61
  209.7 83.0 %all-to-all-start.3 = ((bf16[4,528,384]{2,1,0:T(8,128)(2,1)}), bf16[4,528,384]{2,1,0:T(8,128)(2,1)S(1)}, u32[]{:S(2)}, u32[]{:S(2)}) async-start(bf16[4,528,384]{2,1,0:T(8,128)(2,1)} %normed.1), calls=%async_computation.3 | async-start | bytes 3244032 | tf_op jit(solution)/shard_map/all_to_all | solution.py:57
  220.3 25.3 %collective-permute-start.28 = (bf16[2,192,768]{2,1,0:T(8,128)(2,1)S(1)}, bf16[2,192,768]{2,1,0:T(8,128)(2,1)S(1)}, u32[]{:S(2)}, u32[]{:S(2)}) collective-permute-start(bf16[2,192,768]{2,1,0:T(8,128)(2,1)S(1)} %pad_maximum_fusion.1.refs_4_), channel_id=1, source_target_pairs={{0,16},{8,24},{16,0},{24,8},{1,17},{9,25},{17,1},{25,9},{2,18},{10... | collective-permute-start | bytes 1769480 | tf_op jit(solution)/shard_map/ppermute | solution.py:61
  222.7 18.5 %collective-permute-start.40 = (f32[80,768]{1,0:T(8,128)S(1)}, f32[80,768]{1,0:T(8,128)S(1)}, u32[]{:S(2)}, u32[]{:S(2)}) collective-permute-start(f32[80,768]{1,0:T(8,128)S(1)} %slice.61), channel_id=1, source_target_pairs={{0,1},{1,0},{2,3},{3,2},{4,5},{5,4},{6,7},{7,6},{8,9},{9,8},{10,11... | collective-permute-start | bytes 737288 | tf_op jit(solution)/shard_map/ppermute | solution.py:72
  224.6 29.9 %collective-permute-start.24 = (bf16[2,192,768]{2,1,0:T(8,128)(2,1)S(1)}, bf16[2,192,768]{2,1,0:T(8,128)(2,1)}, u32[]{:S(2)}, u32[]{:S(2)}) collective-permute-start(bf16[2,192,768]{2,1,0:T(8,128)(2,1)S(1)} %pad_maximum_fusion.refs_0_), channel_id=1, source_target_pairs={{0,8},{8,0},{16,24},{24,16},{1,9},{9,1},{17,25},{25,17},{2,10},{10... | collective-permute-start | bytes 1769480 | tf_op jit(solution)/shard_map/ppermute | solution.py:61
  225.6 38.0 %collective-permute-start.27 = (bf16[2,192,768]{2,1,0:T(8,128)(2,1)S(1)}, bf16[2,192,768]{2,1,0:T(8,128)(2,1)S(1)}, u32[]{:S(2)}, u32[]{:S(2)}) collective-permute-start(bf16[2,192,768]{2,1,0:T(8,128)(2,1)S(1)} %pad_maximum_fusion.1.refs_4_), channel_id=1, source_target_pairs={{0,4},{4,0},{1,5},{5,1},{2,6},{6,2},{3,7},{7,3},{8,12},{12,8},{9,1... | collective-permute-start | bytes 1769480 | tf_op jit(solution)/shard_map/ppermute | solution.py:34
  237.3 17.4 %collective-permute-start.46 = (bf16[128,768]{1,0:T(8,128)(2,1)S(1)}, bf16[128,768]{1,0:T(8,128)(2,1)S(1)}, u32[]{:S(2)}, u32[]{:S(2)}) collective-permute-start(bf16[128,768]{1,0:T(8,128)(2,1)S(1)} %get-tuple-element.132), channel_id=1, source_target_pairs={{0,16},{8,24},{16,0},{24,8},{1,17},{9,25},{17,1},{25,9},{2,18},{10... | collective-permute-start | bytes 589832 | tf_op jit(solution)/shard_map/ppermute | solution.py:61
  241.3 21.0 %collective-permute-start.41 = (f32[80,768]{1,0:T(8,128)S(1)}, f32[80,768]{1,0:T(8,128)S(1)}, u32[]{:S(2)}, u32[]{:S(2)}) collective-permute-start(f32[80,768]{1,0:T(8,128)S(1)} %slice_add_fusion.1), channel_id=1, source_target_pairs={{0,2},{1,3},{2,0},{3,1},{4,6},{5,7},{6,4},{7,5},{8,10},{9,11},{10,... | collective-permute-start | bytes 737288 | tf_op jit(solution)/shard_map/ppermute | solution.py:72
  245.6 30.0 %collective-permute-start.23 = (bf16[2,192,768]{2,1,0:T(8,128)(2,1)S(1)}, bf16[2,192,768]{2,1,0:T(8,128)(2,1)S(1)}, u32[]{:S(2)}, u32[]{:S(2)}) collective-permute-start(bf16[2,192,768]{2,1,0:T(8,128)(2,1)S(1)} %pad_maximum_fusion.refs_0_), channel_id=1, source_target_pairs={{0,4},{4,0},{1,5},{5,1},{2,6},{6,2},{3,7},{7,3},{8,12},{12,8},{9,1... | collective-permute-start | bytes 1769480 | tf_op jit(solution)/shard_map/ppermute | solution.py:34
  254.6 21.9 %collective-permute-start.29 = (bf16[2,192,768]{2,1,0:T(8,128)(2,1)S(1)}, bf16[2,192,768]{2,1,0:T(8,128)(2,1)S(1)}, u32[]{:S(2)}, u32[]{:S(2)}) collective-permute-start(bf16[2,192,768]{2,1,0:T(8,128)(2,1)S(1)} %collective-permute-done.28.refs_6_), channel_id=1, source_target_pairs={{0,4},{4,0},{1,5},{5,1},{2,6},{6,2},{3,7},{7,3},{8,12},{12,8},{9,1... | collective-permute-start | bytes 1769480 | tf_op jit(solution)/shard_map/ppermute | solution.py:34
  254.6 25.3 %collective-permute-start.25 = (bf16[2,192,768]{2,1,0:T(8,128)(2,1)}, bf16[2,192,768]{2,1,0:T(8,128)(2,1)}, u32[]{:S(2)}, u32[]{:S(2)}) collective-permute-start(bf16[2,192,768]{2,1,0:T(8,128)(2,1)} %collective-permute-done.24.refs_2_), channel_id=1, source_target_pairs={{0,4},{4,0},{1,5},{5,1},{2,6},{6,2},{3,7},{7,3},{8,12},{12,8},{9,1... | collective-permute-start | bytes 1769480 | tf_op jit(solution)/shard_map/ppermute | solution.py:34
  262.3 17.7 %collective-permute-start.48 = (bf16[2,128,768]{2,1,0:T(8,128)(2,1)}, bf16[2,128,768]{2,1,0:T(8,128)(2,1)}, u32[]{:S(2)}, u32[]{:S(2)}) collective-permute-start(bf16[2,128,768]{2,1,0:T(8,128)(2,1)} %pad_maximum_fusion.2.refs_0_), channel_id=1, source_target_pairs={{0,8},{8,0},{16,24},{24,16},{1,9},{9,1},{17,25},{25,17},{2,10},{10... | collective-permute-start | bytes 1179656 | tf_op jit(solution)/shard_map/ppermute | solution.py:61
  280.0 18.4 %collective-permute-start.47 = (bf16[2,128,768]{2,1,0:T(8,128)(2,1)}, bf16[2,128,768]{2,1,0:T(8,128)(2,1)}, u32[]{:S(2)}, u32[]{:S(2)}) collective-permute-start(bf16[2,128,768]{2,1,0:T(8,128)(2,1)} %pad_maximum_fusion.2.refs_0_), channel_id=1, source_target_pairs={{0,4},{4,0},{1,5},{5,1},{2,6},{6,2},{3,7},{7,3},{8,12},{12,8},{9,1... | collective-permute-start | bytes 1179656 | tf_op jit(solution)/shard_map/ppermute | solution.py:34
  280.0 18.3 %collective-permute-start.49 = (bf16[2,128,768]{2,1,0:T(8,128)(2,1)}, bf16[2,128,768]{2,1,0:T(8,128)(2,1)}, u32[]{:S(2)}, u32[]{:S(2)}) collective-permute-start(bf16[2,128,768]{2,1,0:T(8,128)(2,1)} %collective-permute-done.48.refs_2_), channel_id=1, source_target_pairs={{0,4},{4,0},{1,5},{5,1},{2,6},{6,2},{3,7},{7,3},{8,12},{12,8},{9,1... | collective-permute-start | bytes 1179656 | tf_op jit(solution)/shard_map/ppermute | solution.py:34
  282.3 16.0 %collective-permute-start.53 = (bf16[2,64,768]{2,1,0:T(8,128)(2,1)}, bf16[2,64,768]{2,1,0:T(8,128)(2,1)}, u32[]{:S(2)}, u32[]{:S(2)}) collective-permute-start(bf16[2,64,768]{2,1,0:T(8,128)(2,1)} %collective-permute-done.52.refs_6_), channel_id=1, source_target_pairs={{0,4},{4,0},{1,5},{5,1},{2,6},{6,2},{3,7},{7,3},{8,12},{12,8},{9,1... | collective-permute-start | bytes 589832 | tf_op jit(solution)/shard_map/ppermute | solution.py:34
  285.0 19.0 %collective-permute-start.43 = (bf16[2,80,768]{2,1,0:T(8,128)(2,1)S(1)}, bf16[2,80,768]{2,1,0:T(8,128)(2,1)}, u32[]{:S(2)}, u32[]{:S(2)}) collective-permute-start(bf16[2,80,768]{2,1,0:T(8,128)(2,1)S(1)} %pad_maximum_fusion.3.refs_0_), channel_id=1, source_target_pairs={{0,4},{4,0},{1,5},{5,1},{2,6},{6,2},{3,7},{7,3},{8,12},{12,8},{9,1... | collective-permute-start | bytes 737288 | tf_op jit(solution)/shard_map/ppermute | solution.py:34
  285.0 19.0 %collective-permute-start.45 = (bf16[2,80,768]{2,1,0:T(8,128)(2,1)}, bf16[2,80,768]{2,1,0:T(8,128)(2,1)}, u32[]{:S(2)}, u32[]{:S(2)}) collective-permute-start(bf16[2,80,768]{2,1,0:T(8,128)(2,1)} %collective-permute-done.44.refs_2_), channel_id=1, source_target_pairs={{0,4},{4,0},{1,5},{5,1},{2,6},{6,2},{3,7},{7,3},{8,12},{12,8},{9,1... | collective-permute-start | bytes 737288 | tf_op jit(solution)/shard_map/ppermute | solution.py:34
  (117 other events, 768.7 us)
where the time goes:
time: 313 us; the launch traced here: 311 us
  starting transfers between devices  105 us (34%)
  waiting for transfers between devices  66.4 us (21%)
  Pallas kernels  63.1 us (20%)
  local copies, waits for them, and re-layouts  45.9 us (15%)
  other arithmetic  18.3 us (6%)
  matrix products  10.8 us (3%)
    pallas_call x22, Pallas kernels, run(): pl.pallas_call(kernel, out_shape=shapes, in_specs=[spec(kind, a.shape) fo...  63.1 us
    ppermute x24, waiting for transfers between devices, cross(): lax.ppermute(value, 'chip', [(i, i ^ bits) for i in range(lax.axis_size('...  46.2 us
    unnamed x183, local copies, waits for them, and re-layouts  36.6 us
    ppermute x16, starting transfers between devices, beside(): return lax.ppermute(value, 'core', [(0, 1), (1, 0)])  33.8 us
    ppermute x24, starting transfers between devices, cross(): lax.ppermute(value, 'chip', [(i, i ^ bits) for i in range(lax.axis_size('...  18.3 us
    ppermute x7, starting transfers between devices, turn(): lax.ppermute(value, axis, [(i, (i + by) % size) for i in range(size)])  14.8 us
    all_to_all x3, starting transfers between devices, deal(): return lax.all_to_all(parts, axis, 0, 0)  13.9 us
    dot_general x3, matrix products, dot(): return jnp.dot(left, right, preferred_element_type=F32)  9.35 us
  transfers between devices with their start and end apart: 58, of which 19 were waited for; matrix products, arithmetic and copies ran while one was open for 11% of the time, Pallas kernels for 15%

commit v1 on v0

--- a/solution.py
+++ b/solution.py
@@ -13,7 +13,8 @@
 KERNEL = 4
 CHUNK = 128
 BLOCK = 384
-VMEM_LIMIT = 20 * 1024 * 1024
+VMEM_LIMIT = 56 * 1024 * 1024
+MARGIN = 32
 HALO = 16
 
 
@@ -21,6 +22,21 @@
 EPSILON = 1e-05
 BF16 = jnp.bfloat16
 F32 = jnp.float32
+
+
+def tie_kernel(*refs):
+    del refs
+
+
+def tie(value, *others):
+    return pl.pallas_call(
+        tie_kernel,
+        out_shape=jax.ShapeDtypeStruct(value.shape, value.dtype),
+        in_specs=[pl.BlockSpec(memory_space=pl.ANY)] * (1 + len(others)),
+        out_specs=pl.BlockSpec(memory_space=pl.ANY),
+        input_output_aliases={0: 0},
+        name="tie",
+    )(value, *others)
 
 
 def from_behind(value, by):
@@ -43,10 +59,10 @@
     return [value] + [turn(value, axis, by) for by in range(1, lax.axis_size(axis))]
 
 
-def line_parts(value, axis):
+def line_parts(value, axis, meanwhile):
     if lax.axis_size(axis) != 4:
         return turn_all(value, axis), value
-    two = turn(value, axis, 2)
+    two = tie(turn(value, axis, 2), meanwhile)
     one = lax.ppermute(value, axis, [(0, 1), (1, 2), (2, 3)])
     three = lax.ppermute(value, axis, [(1, 0), (2, 1), (3, 2)])
     passed = lax.ppermute(two, axis, [(2, 3), (1, 0)])
@@ -74,47 +90,38 @@
     return value
 
 
-def decay_weights(logs, backward):
-    chips, mine = lax.axis_size("chip"), lax.axis_index("chip")
-    source = (jnp.arange(chips) ^ mine)[:, None]
-    middle = jnp.arange(chips)[None, :]
-    if backward:
-        between, passes = (middle < source) & (middle > mine), source > mine
-    else:
-        between, passes = (middle > source) & (middle < mine), source < mine
-    spans = jnp.sum(jnp.where(between[:, :, None], logs[None], 0.0), axis=1)
-    return jnp.where(passes, jnp.exp(spans), 0.0)
-
-
-def entering(total, own_decay, other_decay, weights, backward):
+def entering(total, weights, first_row, backward, meanwhile):
     core = lax.axis_index("core")
     receives = core == (0 if backward else 1)
+    own_decay, other_decay = weights[16:17], weights[17:18]
     half = total.shape[0] // 2
-    partner = beside(total)
+    partner = tie(beside(total), meanwhile)
     part = lambda value: lax.dynamic_slice_in_dim(value, core * half, half, 0)
     pair = jnp.where(
         receives,
         own_decay * part(partner) + part(total),
         other_decay * part(total) + part(partner),
     )
-    prefix = jnp.zeros_like(pair)
+    prefix, mark = jnp.zeros_like(pair), None
     for bits in range(1, lax.axis_size("chip")):
-        prefix = prefix + cross(pair, bits) * weights[bits : bits + 1]
+        arrived = cross(pair, bits)
+        mark = arrived if mark is None else mark
+        prefix = prefix + arrived * weights[first_row + bits : first_row + bits + 1]
     other = beside(prefix)
     whole = jnp.where(
         core == 0,
         jnp.concatenate([prefix, other], axis=0),
         jnp.concatenate([other, prefix], axis=0),
     )
-    return jnp.where(receives, other_decay * whole + partner, whole), pair
-
-
-def sum_pieces(chip, kept, given, cut, paired, name):
+    return jnp.where(receives, other_decay * whole + partner, whole), mark
+
+
+def sum_pieces(chip, kept, given, cut, paired, name, square):
     chips, rows, channels = kept.shape
     arrived = beside(given)
     rest = rows - cut
     size = chips * rows * channels
-    if chips != 4:
+    if chips != 4 or not square:
         halves = run(
             functools.partial(half_kernel, paired, chips), name + "_half", size,
             [chip, (WHOLE, kept), (WHOLE, arrived)],
@@ -126,7 +133,7 @@
             [(WHOLE, part) for part in parts],
             [(WHOLE, (cut, channels), BF16), (WHOLE, (rest, channels), F32 if paired else BF16)],
         )
-        return first, last, halves[0]
+        return first, last, halves[0], halves[0]
     first, first_give, last, last_give = run(
         functools.partial(square_half_kernel, paired), name + "_half", size,
         [chip, (WHOLE, kept), (WHOLE, arrived)],
@@ -135,7 +142,7 @@
             (WHOLE, (2, rest, channels), F32), (WHOLE, (2, rest, channels), BF16),
         ],
     )
-    mark = first
+    half_mark = first
     first, first_give, last, last_give = run(
         functools.partial(square_next_kernel, paired), name + "_next", size,
         [
@@ -147,6 +154,7 @@
             (WHOLE, (rest, channels), F32), (WHOLE, (rest, channels), BF16),
         ],
     )
+    next_mark = first
     first, last = run(
         functools.partial(square_last_kernel, paired), name + "_piece", size,
         [
@@ -155,12 +163,12 @@
         ],
         [(WHOLE, (cut, channels), BF16), (WHOLE, (rest, channels), F32 if paired else BF16)],
     )
-    return first, last, mark
+    return first, last, half_mark, next_mark
 
 
 def collect(piece, order):
     chips = lax.axis_size("chip")
-    if chips != 4:
+    if chips != 4 or order is None:
         found = [(value[None], (bits,)) for bits, value in enumerate(cross_all(piece))]
     else:
         near, far = order
@@ -192,7 +200,7 @@
     return row >= column
 
 
-def decay_kernel(codes_ref, weight_ref, e_ref, f_ref, k_ref):
+def decay_kernel(codes_ref, weight_ref, e_ref, f_ref, k_ref, logs_ref):
     heads, channels = codes_ref.shape[1], e_ref.shape[1]
     row = lax.broadcasted_iota(jnp.int32, (heads, channels), 0)
     column = lax.broadcasted_iota(jnp.int32, (heads, channels), 1)
@@ -223,7 +231,33 @@
     marks = jnp.where(line == 7, total, marks)
     high, low = split(marks)
     lowest = (marks - high.astype(F32) - low.astype(F32)).astype(BF16)
-    k_ref[...] = dot(high, spread) + dot(low, spread) + dot(lowest, spread)
+    factors = dot(high, spread) + dot(low, spread) + dot(lowest, spread)
+    k_ref[...] = factors
+    for place in range(logs_ref.shape[0]):
+        logs_ref[place] = jnp.broadcast_to(factors[7:8], (8, channels))
+
+
+def weights_kernel(core_ref, chip_ref, logs_ref, out_ref):
+    chips = logs_ref.shape[0] // 2
+    core, chip = core_ref[0], chip_ref[0]
+    logs = [logs_ref[i, 0:1, :] for i in range(2 * chips)]
+    pairs = [logs[2 * i] + logs[2 * i + 1] for i in range(chips)]
+    zero = jnp.zeros_like(logs[0])
+    out_ref[...] = jnp.zeros_like(out_ref)
+    for bits in range(1, chips):
+        source = lax.bitwise_xor(chip, bits)
+        before, after = zero, zero
+        for middle in range(chips):
+            before = before + jnp.where((source < middle) & (middle < chip), pairs[middle], 0.0)
+            after = after + jnp.where((source > middle) & (middle > chip), pairs[middle], 0.0)
+        out_ref[bits : bits + 1, :] = jnp.where(source < chip, jnp.exp(before), 0.0)
+        out_ref[8 + bits : 9 + bits, :] = jnp.where(source > chip, jnp.exp(after), 0.0)
+    own, other = zero, zero
+    for device in range(2 * chips):
+        own = own + jnp.where(2 * chip + core == device, logs[device], 0.0)
+        other = other + jnp.where(2 * chip + 1 - core == device, logs[device], 0.0)
+    out_ref[16:17, :] = jnp.exp(own)
+    out_ref[17:18, :] = jnp.exp(other)
 
 
 def taps(window, kernel, bias, begin):
@@ -268,40 +302,28 @@
 
 
 def norm_kernel(size, head_ref, passed_ref, *refs):
-    parts, margins, (own_ref,) = refs[:size], refs[size : 2 * size], refs[2 * size : 2 * size + 1]
-    normed_ref, full_ref, gain_ref, scale_ref, copy_ref = refs[2 * size + 1 : 2 * size + 6]
-    head_normed, = refs[2 * size + 6 :]
+    parts, gains = refs[:size], refs[size : 2 * size]
+    passed_gain_ref, own_ref, normed_ref, scale_ref, copy_ref, gain_ref = refs[2 * size :]
     width = parts[0].shape[1]
     mine = head_ref[0]
 
-    def part(i):
+    def pick(i, refs, passed):
         if size == 4 and i == 1:
-            return jnp.where(mine == 0, passed_ref[...], parts[i][...])
+            return jnp.where(mine == 0, passed[...], refs[i][...])
         if size == 4 and i == 3:
-            return jnp.where(mine == 3, passed_ref[...], parts[i][...])
-        return parts[i][...]
-
-    def scale_of(values):
-        squares = sum(jnp.sum(value.astype(F32) ** 2, axis=1, keepdims=True) for value in values)
-        return lax.rsqrt(squares / (size * width) + EPSILON)
-
-    scale = scale_of(part(i) for i in range(size))
+            return jnp.where(mine == 3, passed[...], refs[i][...])
+        return refs[i][...]
+
+    part = lambda i: pick(i, parts, passed_ref).astype(F32)
+    gain = lambda i: pick(i, gains, passed_gain_ref)[0:1].astype(F32)
+    squares = sum(jnp.sum(part(i) ** 2, axis=1, keepdims=True) for i in range(size))
+    scale = lax.rsqrt(squares / (size * width) + EPSILON)
     scale_ref[...] = jnp.broadcast_to(scale, scale_ref.shape)
-    ahead = scale_of(ref[:HALO] for ref in margins)
-    gain = lambda i: margins[i][HALO : HALO + 1, :].astype(F32)
     place_parts(
-        mine, margins, head_normed, width,
-        lambda i: (margins[i][:HALO].astype(F32) * ahead * gain(i)).astype(BF16),
-    )
-    place_parts(
-        mine, parts, normed_ref.at[HALO:], width,
-        lambda i: (part(i).astype(F32) * scale_ref[:, 0:1] * gain(i)).astype(BF16),
-    )
-    normed_ref[:HALO, :] = head_normed[...]
-    place_parts(mine, parts, full_ref, width, part)
-    place_parts(
-        mine, margins, gain_ref, width, lambda i: jnp.broadcast_to(gain(i), (8, width))
-    )
+        mine, parts, normed_ref, width,
+        lambda i: (part(i) * scale_ref[:, 0:1] * gain(i)).astype(BF16),
+    )
+    place_parts(mine, parts, gain_ref, width, lambda i: jnp.broadcast_to(gain(i), (8, width)))
     for i in range(size):
         copy_ref[i] = own_ref[...]
 
@@ -379,13 +401,18 @@
     return jnp.concatenate([row_block, rest], axis=0).T
 
 
+def row_of(sums):
+    lane = lax.broadcasted_iota(jnp.int32, (CHUNK, CHUNK), 1)
+    return jnp.where(lane == 0, sums, 0.0).T[:8]
+
+
 def gate_kernel(
     inner, chunks, size, *refs
 ):
     stats_refs = refs[:size]
     (
         mixer_ref, gate_ref, grad_ref, gain_ref, conv_ref, e_ref, k_ref, maps_ref,
-        mixed_ref, gate_grad_ref, mixer_grad_ref, small_ref, total_ref,
+        mixed_ref, gate_grad_ref, mixer_grad_ref, small_ref, total_ref, cross_ref,
     ) = refs[size:]
     chunk = chunks - 1 - pl.program_id(0)
     clear(small_ref, total_ref)
@@ -393,14 +420,17 @@
     stats = column(sum(ref[...] for ref in stats_refs))
     scale = lax.rsqrt(stats[:, 0:1] / inner + EPSILON)
     cross_term = stats[:, 1:2] * (scale * scale * scale) / inner
-    silu, slope = silu_parts(gate_ref[...])
+    gate = gate_ref[...]
+    silu, slope = silu_parts(gate)
     mixer = mixer_ref[...]
     gated = mixer * silu
     normed = gated * scale
     mixed_ref[...] = (normed * gain).astype(BF16)
     grad = grad_ref[...]
     gated_grad = scale * (grad * gain) - gated * cross_term
-    gate_grad_ref[...] = (gated_grad * mixer * slope).astype(BF16)
+    gate_grad = (gated_grad * mixer * slope).astype(BF16)
+    gate_grad_ref[...] = gate_grad
+    cross_ref[...] = row_of(jnp.sum(gate_grad.astype(F32) * gate, axis=1, keepdims=True))
     mixer_grad = gated_grad * silu
     mixer_grad_ref[...] = mixer_grad
     small_ref[0:1, :] += jnp.sum(grad * normed, axis=0, keepdims=True)
@@ -453,8 +483,9 @@
 
 def conv_back_kernel(
     chunks, other_ref, value_ref, map_ref, after_ref, value_raw_ref, state_raw_ref, value_kernel_ref,
-    state_kernel_ref,
-    value_grad_ref, state_grad_ref, value_small_ref, state_small_ref, value_next_ref, state_next_ref,
+    state_kernel_ref, cross_in_ref,
+    value_grad_ref, state_grad_ref, value_small_ref, state_small_ref, cross_ref, value_next_ref,
+    state_next_ref,
 ):
     chunk = chunks - 1 - pl.program_id(0)
     channels = value_ref.shape[1]
@@ -481,11 +512,16 @@
                 slope * raw[begin : begin + CHUNK], axis=0, keepdims=True
             )
         small_ref[KERNEL : KERNEL + 1, :] += jnp.sum(slope, axis=0, keepdims=True)
-        grad_ref[...] = grad.astype(BF16)
+        grad = grad.astype(BF16)
+        grad_ref[...] = grad
         next_ref[...] = slope[:8]
-
-    back(map_ref, state_next_ref, state_raw_ref, state_kernel_ref, state_grad_ref, state_small_ref)
-    back(value_ref, value_next_ref, value_raw_ref, value_kernel_ref, value_grad_ref, value_small_ref)
+        return jnp.sum(grad.astype(F32) * raw[HALO:], axis=1, keepdims=True)
+
+    crossed = back(map_ref, state_next_ref, state_raw_ref, state_kernel_ref, state_grad_ref, state_small_ref)
+    crossed = crossed + back(
+        value_ref, value_next_ref, value_raw_ref, value_kernel_ref, value_grad_ref, value_small_ref
+    )
+    cross_ref[...] = cross_in_ref[...] + row_of(crossed)
 
 
 def out_kernel(pair_ref, mixed_ref, weight_ref, out_ref):
@@ -496,36 +532,25 @@
 
 
 def normed_kernel(
-    late_ref, gate_grad_ref, value_grad_ref, state_grad_ref, gate_weight_ref, value_weight_ref,
-    state_weight_ref, full_ref, gain_ref, out_ref
+    chunks, late_ref, gate_grad_ref, value_grad_ref, state_grad_ref, gate_weight_ref, value_weight_ref,
+    state_weight_ref, cross_ref, out_ref
 ):
-    size, _, width = out_ref.shape
-    count = full_ref.shape[0]
-    crossed = jnp.zeros((count, 1), F32)
-    for owner in range(size):
-        own = slice(owner * width, (owner + 1) * width)
-        value = (
-            dot_nt(gate_grad_ref[...], gate_weight_ref[own, :])
-            + dot_nt(value_grad_ref[...], value_weight_ref[own, :])
-            + dot_nt(state_grad_ref[...], state_weight_ref[own, :])
-        )
-        weighed = value * full_ref[:, own].astype(F32) * gain_ref[0:1, own]
-        crossed = crossed + jnp.sum(weighed, axis=1, keepdims=True)
-        out_ref[owner, :count, :] = value.astype(BF16)
-
-    chunks = count // CHUNK
+    value = (
+        dot_nt(gate_grad_ref[...], gate_weight_ref[...])
+        + dot_nt(value_grad_ref[...], value_weight_ref[...])
+        + dot_nt(state_grad_ref[...], state_weight_ref[...])
+    )
+    count = value.shape[0]
+    out_ref[0, :count, :] = value.astype(BF16)
     line = lax.broadcasted_iota(jnp.int32, (HALO, CHUNK), 0)
-    lane = lax.broadcasted_iota(jnp.int32, (CHUNK, CHUNK), 1)
     packed = jnp.zeros((HALO, CHUNK), F32)
     for chunk in range(chunks):
-        sums = crossed[chunk * CHUNK : (chunk + 1) * CHUNK]
-        row = jnp.where(lane == 0, sums, 0.0).T[0:1]
+        row = cross_ref[0:1, chunk * CHUNK : (chunk + 1) * CHUNK]
         high = row.astype(BF16).astype(F32)
         packed = jnp.where(line == chunk, high, packed)
         packed = jnp.where(line == chunks + chunk, row - high, packed)
-    for owner in range(size):
-        out_ref[owner, count:, :] = jnp.zeros((HALO, width), BF16)
-        out_ref[owner, count:, :CHUNK] = packed.astype(BF16)
+    out_ref[0, count:, :] = jnp.zeros((HALO, value.shape[1]), BF16)
+    out_ref[0, count:, :CHUNK] = packed.astype(BF16)
 
 
 def last_kernel(full_width, loose_ref, parts_ref, tokens_ref, scale_ref, gain_ref, cotangent_ref, out_ref):
@@ -537,27 +562,28 @@
     for chunk in range(chunks):
         rows = slice(chunk * CHUNK, (chunk + 1) * CHUNK)
         normed_grad = sum(parts_ref[i, rows, :].astype(F32) for i in range(size))
-        scale = scale_ref[rows, 0:1]
+        scale = scale_ref[HALO + chunk * CHUNK : HALO + (chunk + 1) * CHUNK, 0:1]
         total = column(jnp.broadcast_to(crossed[chunk : chunk + 1], (8, CHUNK)))[:, 0:1]
         out_ref[rows, :] = (
             scale * gain_ref[...].astype(F32) * normed_grad
-            - tokens_ref[rows, :].astype(F32) * (scale * scale * scale * total / full_width)
+            - tokens_ref[rows, :].astype(F32) * (scale * scale * total / full_width)
             + cotangent_ref[rows, :].astype(F32)
         ).astype(BF16)
 
 
-def store_piece(core_ref, kept_ref, given_ref, place, piece):
+def store_piece(core_ref, kept_ref, given_ref, place, begin, piece):
     chips = kept_ref.shape[0]
-    core, chip = divmod(place, chips)
+    core, chip = place // chips, lax.rem(place, chips)
+    rows = slice(begin, begin + piece.shape[0])
     piece = piece.astype(BF16)
 
     @pl.when(core_ref[0] == core)
     def _():
-        kept_ref[chip] = piece
+        kept_ref[chip, rows, :] = piece
 
     @pl.when(core_ref[0] != core)
     def _():
-        given_ref[chip] = piece
+        given_ref[chip, rows, :] = piece
 
 
 def gain_row(weight, block):
@@ -570,79 +596,87 @@
 
 
 def early_kernel(
-    pair_ref, core_ref, normed_ref, gate_ref, mixed_ref, grad_ref, weight_ref,
+    loose_ref, core_ref, normed_ref, gate_ref, mixed_ref, grad_ref, weight_ref,
     kept_ref, given_ref, gain_ref, held_ref
 ):
     chips, rows, channels = kept_ref.shape
-    width = normed_ref.shape[1]
+    at = pl.program_id(0)
+    count, width = grad_ref.shape
     pieces = 2 * chips
     step = width // pieces
     out_rows = channels // pieces
-    for begin in range(0, channels, BLOCK):
-        held_ref[begin : begin + BLOCK, :] = dot_tn(mixed_ref[:, begin : begin + BLOCK], grad_ref[...])
-    for begin in range(0, width, BLOCK):
-        block = dot_tn(normed_ref[HALO:, begin : begin + BLOCK], gate_ref[...])
-        gain_ref[0:1, begin : begin + BLOCK] = gain_row(weight_ref[begin : begin + BLOCK, :], block)
-        for place in range(begin // step, (begin + BLOCK) // step):
-            own = held_ref[place * out_rows : (place + 1) * out_rows, :]
-            parts = [block[place * step - begin : (place + 1) * step - begin]]
-            parts += [own[:, i : i + channels] for i in range(0, width, channels)]
-            store_piece(core_ref, kept_ref, given_ref, place, jnp.concatenate(parts, axis=0))
+    out_blocks = channels // BLOCK
+    every = width // BLOCK // out_blocks
+
+    @pl.when(lax.rem(at, every) == 0)
+    def _():
+        held_ref[...] = dot_tn(mixed_ref[...], grad_ref[...])
+
+    block = dot_tn(normed_ref[HALO : HALO + count, :], gate_ref[...])
+    gain_ref[...] = gain_row(weight_ref[...], block)
+    for i in range(BLOCK // step):
+        place = at * (BLOCK // step) + i
+        begin = lax.rem(at, every) * (BLOCK // step * out_rows) + i * out_rows
+        own = held_ref[pl.ds(pl.multiple_of(begin, 8), out_rows), :]
+        parts = [block[i * step : (i + 1) * step]]
+        parts += [own[:, j : j + channels] for j in range(0, width, channels)]
+        store_piece(core_ref, kept_ref, given_ref, place, 0, jnp.concatenate(parts, axis=0))
 
 
 def late_kernel(
     core_ref, normed_ref, value_ref, state_ref, value_small_ref, gate_small_ref, gain_ref,
     state_small_ref, value_weight_ref, state_weight_ref, gain_full_ref,
-    kept_ref, given_ref, own_ref, shared_ref, gains_ref, blocks_ref,
+    kept_ref, given_ref, own_ref, shared_ref, gains_ref,
 ):
     chips, rows, channels = kept_ref.shape
-    width, maps_width = normed_ref.shape[1], state_ref.shape[1]
+    at = pl.program_id(0)
+    count, maps_width = state_ref.shape
+    width = gains_ref.shape[1]
     pieces = 2 * chips
     step = width // pieces
     lanes = channels // 128
-    own_ref[...] = jnp.zeros_like(own_ref)
-    own_ref[: KERNEL + 1, :] = value_small_ref[: KERNEL + 1, :]
-    own_ref[KERNEL + 1 : KERNEL + 3, :] = gate_small_ref[:2, :]
-    for begin in range(0, width, BLOCK):
-        block = slice(begin, begin + BLOCK)
-        columns = normed_ref[HALO:, block]
-        value = dot_tn(columns, value_ref[...])
-        state = dot_tn(columns, state_ref[...])
-        blocks_ref[block, :channels] = value
-        blocks_ref[block, channels:] = state
-        gains_ref[0:1, block] = (
-            gain_ref[0:1, block]
-            + gain_row(value_weight_ref[block, :], value)
-            + gain_row(state_weight_ref[block, :], state)
-        ) / gain_full_ref[0:1, block]
-    shared_ref[...] = jnp.zeros_like(shared_ref)
-    for i in range(width // channels):
-        shared_ref[i : i + 1, :] = gains_ref[0:1, i * channels : (i + 1) * channels]
-    begin = width // channels
-    for i in range(0, (KERNEL + 1) * maps_width, 128):
-        tap, column_from = divmod(i, maps_width)
-        row, column_to = divmod(i, channels)
-        shared_ref[begin + row : begin + row + 1, column_to : column_to + 128] = state_small_ref[
-            tap : tap + 1, column_from : column_from + 128
-        ]
-    line = lax.broadcasted_iota(jnp.int32, (HALO, channels), 0)
     part = 2 * step // lanes
-    for place in range(pieces):
-        piece = blocks_ref[place * step : (place + 1) * step, :]
-        state = piece[:, channels:]
-        stacked = jnp.concatenate([state[:, :128], state[:, 128:]], axis=0)
+    columns = normed_ref[HALO : HALO + count, :]
+    value = dot_tn(columns, value_ref[...])
+    state = dot_tn(columns, state_ref[...])
+    gain = (
+        gain_ref[...] + gain_row(value_weight_ref[...], value) + gain_row(state_weight_ref[...], state)
+    ) / gain_full_ref[0:1, :]
+    gains_ref[0:1, pl.ds(pl.multiple_of(at * BLOCK, 128), BLOCK)] = gain
+    for i in range(BLOCK // step):
+        piece = slice(i * step, (i + 1) * step)
+        stacked = jnp.concatenate([state[piece, :128], state[piece, 128:]], axis=0)
         stacked = jnp.concatenate(
-            [stacked[i * part : (i + 1) * part] for i in range(lanes)], axis=1
+            [stacked[j * part : (j + 1) * part] for j in range(lanes)], axis=1
         )
-        own, shared = own_ref[place : place + 1, :], shared_ref[place : place + 1, :]
-        own_high, shared_high = (v.astype(BF16).astype(F32) for v in (own, shared))
-        small = jnp.zeros((HALO, channels), F32)
-        for at, line_value in enumerate((own_high, own - own_high, shared_high, shared - shared_high)):
-            small = jnp.where(line == at, line_value, small)
         store_piece(
-            core_ref, kept_ref, given_ref, place,
-            jnp.concatenate([piece[:, :channels], stacked, small], axis=0),
+            core_ref, kept_ref, given_ref, at * (BLOCK // step) + i, 0,
+            jnp.concatenate([value[piece], stacked], axis=0),
         )
+
+    @pl.when(at == width // BLOCK - 1)
+    def _():
+        own_ref[...] = jnp.zeros_like(own_ref)
+        own_ref[: KERNEL + 1, :] = value_small_ref[: KERNEL + 1, :]
+        own_ref[KERNEL + 1 : KERNEL + 3, :] = gate_small_ref[:2, :]
+        shared_ref[...] = jnp.zeros_like(shared_ref)
+        begin = width // channels
+        for i in range(begin):
+            shared_ref[i : i + 1, :] = gains_ref[0:1, i * channels : (i + 1) * channels]
+        for i in range(0, (KERNEL + 1) * maps_width, 128):
+            tap, column_from = divmod(i, maps_width)
+            row, column_to = divmod(i, channels)
+            shared_ref[begin + row : begin + row + 1, column_to : column_to + 128] = state_small_ref[
+                tap : tap + 1, column_from : column_from + 128
+            ]
+        line = lax.broadcasted_iota(jnp.int32, (HALO, channels), 0)
+        for place in range(pieces):
+            own, shared = own_ref[place : place + 1, :], shared_ref[place : place + 1, :]
+            own_high, shared_high = (v.astype(BF16).astype(F32) for v in (own, shared))
+            small = jnp.zeros((HALO, channels), F32)
+            for to, value in enumerate((own_high, own - own_high, shared_high, shared - shared_high)):
+                small = jnp.where(line == to, value, small)
+            store_piece(core_ref, kept_ref, given_ref, place, step + part, small)
 
 
 def merge_pairs(block):
@@ -743,14 +777,11 @@
     spread_pieces(core_ref, chip_ref, chips, groups, refs[:-2], store)
 
 
-def late_out_kernel(chips, groups, cut, core_ref, chip_ref, *refs):
+def late_out_kernel(chips, groups, core_ref, chip_ref, *refs):
     value_ref = refs[-1]
 
     def store(part, value):
-        if part == 0:
-            value_ref[:cut, :] = value
-        else:
-            value_ref[cut:, :] = value
+        value_ref[...] = value
 
     spread_pieces(core_ref, chip_ref, chips, groups, refs[:-1], store)
 
@@ -803,7 +834,7 @@
 LOOSE = "loose"
 
 
-def run(kernel, name, flops, args, outs, steps=None, backward=False, scratch=()):
+def run(kernel, name, flops, args, outs, steps=1, backward=False, scratch=()):
     at = (lambda i: steps - 1 - i) if backward else (lambda i: i)
 
     def spec(kind, shape):
@@ -813,8 +844,8 @@
             return pl.BlockSpec(memory_space=pltpu.SMEM)
         if kind == LOOSE:
             return pl.BlockSpec(memory_space=pl.ANY)
-        if steps is None:
-            return pl.BlockSpec(memory_space=pltpu.VMEM)
+        if isinstance(kind, tuple):
+            return pl.BlockSpec(*kind)
         if kind == BLOCKED:
             return pl.BlockSpec((CHUNK, shape[1]), lambda i: (at(i), 0))
         if kind == LANES:
@@ -835,7 +866,7 @@
         compiler_params=pltpu.CompilerParams(vmem_limit_bytes=VMEM_LIMIT),
         cost_estimate=pl.CostEstimate(flops=flops, bytes_accessed=moved, transcendentals=0),
         name=name,
-        **({} if steps is None else {"grid": (steps,)}),
+        grid=(steps,),
     )(*(a for _, a in args))
 
 
@@ -856,45 +887,52 @@
     chip = (SCALAR, lax.axis_index("chip").astype(jnp.int32)[None])
     head = (SCALAR, lax.axis_index("head").astype(jnp.int32)[None])
 
-    parts, passed = line_parts(tokens, "head")
-    before = from_behind(tokens[-HALO:], 1)
-    margins = turn_all(
-        jnp.concatenate([before, jnp.broadcast_to(norm_gain[None], (HALO, own_width))], axis=0),
-        "head",
+    rows = count + MARGIN
+    packed = jnp.concatenate(
+        [
+            from_behind(tokens[-HALO:], 1),
+            tokens,
+            jnp.broadcast_to(norm_gain[None], (MARGIN - HALO, own_width)),
+        ],
+        axis=0,
     )
     logs = decay_codes.astype(F32) * (-DECAY_STEP)
     input_weight = jnp.sqrt(-jnp.expm1(2.0 * logs))
-    e_full, f_full, factors = run(
+    e_full, f_full, factors, all_logs = run(
         decay_kernel, "decays", count * channels * 200,
         [(WHOLE, decay_codes), (WHOLE, input_weight)],
         [
             (WHOLE, (count, channels), F32),
             (WHOLE, (count, channels), F32),
             (WHOLE, (8, channels), F32),
-        ],
-    )
-    all_logs = lax.all_to_all(
-        jnp.broadcast_to(factors[None], (seq_size, 8, channels)), ("chip", "core"), 0, 0
-    )[:, 7].reshape(chips, 2, channels)
-    pair_logs = jnp.sum(all_logs, axis=1)
-    own_logs = lax.dynamic_index_in_dim(all_logs, lax.axis_index("chip"), 0, keepdims=False)
-    own_decay = jnp.exp(lax.dynamic_index_in_dim(own_logs, lax.axis_index("core"), 0))
-    other_decay = jnp.exp(lax.dynamic_index_in_dim(own_logs, 1 - lax.axis_index("core"), 0))
-    before_weights = decay_weights(pair_logs, False)
-    after_weights = decay_weights(pair_logs, True)
+            (WHOLE, (seq_size, 8, channels), F32),
+        ],
+    )
+    all_logs = lax.all_to_all(all_logs, ("chip", "core"), 0, 0)
+    weights = run(
+        weights_kernel, "weights", channels * 1000, [core, chip, (WHOLE, all_logs)],
+        [(WHOLE, (24, channels), F32)],
+    )[0]
+    parts, passed = line_parts(packed, "head", weights)
     skip_full = jnp.repeat(skip_scale, HEAD_DIM)[None]
 
-    normed, full, gain_full, scale_in, cotangent_copy = run(
+    half = rows // 2
+    gain_rows = ((MARGIN - HALO, own_width), lambda i: ((HALO + count) // (MARGIN - HALO), 0))
+    normed, scale_in, cotangent_copy, gain_full = run(
         functools.partial(norm_kernel, head_size), "norm", count * width * 10,
-        [head] + [(WHOLE, a) for a in [passed] + parts + margins + [cotangent]],
-        [
-            (WHOLE, (HALO + count, width), BF16),
-            (WHOLE, (count, width), BF16),
+        [head, (half, passed)] + [(half, part) for part in parts]
+        + [(gain_rows, part) for part in parts]
+        + [(gain_rows, passed), (count // 2, cotangent)],
+        [
+            (half, (rows, width), BF16),
+            (half, (rows, 128), F32),
+            (
+                ((head_size, count // 2, own_width), lambda i: (0, i, 0)),
+                (head_size, count, own_width), BF16,
+            ),
             (WHOLE, (8, width), F32),
-            (WHOLE, (count, 128), F32),
-            (WHOLE, (head_size, count, own_width), BF16),
-        ],
-        scratch=[pltpu.VMEM((HALO, width), BF16)],
+        ],
+        steps=2,
     )
     cotangent_parts = deal(cotangent_copy, "head")
     value_raw = dot(normed, value_weight).astype(BF16)
@@ -915,8 +953,8 @@
         ],
         steps=chunks,
     )
-    state_in, _ = entering(local_end, own_decay, other_decay, before_weights, False)
-    gate_pre = dot(normed[HALO:], gate_weight)
+    gate_pre = dot(normed, gate_weight)[HALO : HALO + count]
+    state_in, _ = entering(local_end, weights, 0, False, gate_pre)
     full_cotangent = run(
         place_kernel, "place", count * width, [(WHOLE, cotangent_parts)],
         [(WHOLE, (count, width), BF16)],
@@ -938,7 +976,7 @@
         steps=chunks,
         scratch=[pltpu.VMEM((NSTATE, channels), F32)],
     )
-    mixed, gate_grad, mixer_grad, gate_small, start_grad = run(
+    mixed, gate_grad, mixer_grad, gate_small, start_grad, gate_cross = run(
         functools.partial(gate_kernel, float(channels * head_size), chunks, head_size),
         "gate", count * channels * 600,
         [(LANES, part) for part in turn_all(stats, "head")]
@@ -952,30 +990,36 @@
             (BLOCKED, (count, channels), F32),
             (WHOLE, (8, channels), F32),
             (WHOLE, (NSTATE, channels), F32),
+            (LANES, (8, count), F32),
         ],
         steps=chunks,
         backward=True,
     )
-    grad_after, pair = entering(start_grad, own_decay, other_decay, after_weights, True)
-
     out_parts = run(
         out_kernel, "out", 2 * count * channels * width,
         [(LOOSE, start_grad), (WHOLE, mixed), (WHOLE, output_weight)],
         [(WHOLE, (head_size, count, own_width), BF16)],
     )[0]
+    grad_after, mark = entering(start_grad, weights, 8, True, out_parts)
     step, out_rows = width // seq_size, channels // seq_size
-    rows = step + out_rows * (width // channels)
+    early_rows = step + out_rows * (width // channels)
+    features = width // BLOCK
+    feature_block = ((rows, BLOCK), lambda i: (0, i))
+    every = features // (channels // BLOCK)
     early_kept, early_given, early_gain = run(
         early_kernel, "early", 4 * count * channels * width,
         [
-            (LOOSE, pair), core, (WHOLE, normed), (WHOLE, gate_grad), (WHOLE, mixed),
-            (WHOLE, full_cotangent), (WHOLE, gate_weight),
-        ],
-        [(WHOLE, (chips, rows, channels), BF16)] * 2 + [(WHOLE, (1, width), F32)],
-        scratch=[pltpu.VMEM((channels, width), F32)],
-    )
-    early_gate, early_out, early_mark = sum_pieces(
-        chip, early_kept, early_given, step, False, "early"
+            (LOOSE, mark), core, (feature_block, normed), (WHOLE, gate_grad),
+            (((count, BLOCK), lambda i: (0, i // every)), mixed), (WHOLE, full_cotangent),
+            (BLOCK, gate_weight),
+        ],
+        [(WHOLE, (chips, early_rows, channels), BF16)] * 2
+        + [(((1, BLOCK), lambda i: (0, i)), (1, width), F32)],
+        steps=features,
+        scratch=[pltpu.VMEM((BLOCK, width), F32)],
+    )
+    early_gate, early_out, half_mark, next_mark = sum_pieces(
+        chip, early_kept, early_given, step, False, "early", True
     )
     branch = jnp.sum(deal(out_parts, "head").astype(F32), axis=0)
     block_out = (tokens.astype(F32) + branch).astype(BF16)
@@ -983,7 +1027,7 @@
     value_grads, map_grads = run(
         functools.partial(back_kernel, chunks), "back", count * channels * 2000,
         [
-            (LOOSE, early_given), (LOOSE, out_parts), (WHOLE, grad_after), (BLOCKED, mixer_grad), (BLOCKED, e_full),
+            (LOOSE, half_mark), (LOOSE, out_parts), (WHOLE, grad_after), (BLOCKED, mixer_grad), (BLOCKED, e_full),
             (BLOCKED, f_full), (WHOLE, factors), (BLOCKED, weighted), (LEADING, high),
             (LEADING, low), (BLOCKED, maps), (BLOCKED, value_slope), (BLOCKED, map_slope),
             (WHOLE, skip_full),
@@ -994,17 +1038,19 @@
         scratch=[pltpu.VMEM((NSTATE, channels), F32)],
     )
     after = from_behind(jnp.concatenate([value_grads[:8], map_grads[:8]], axis=1), -1)
-    value_raw_grad, state_raw_grad, value_small, state_small = run(
+    value_raw_grad, state_raw_grad, value_small, state_small, crossed = run(
         functools.partial(conv_back_kernel, chunks), "conv_back", count * channels * 100,
         [
-            (LOOSE, early_mark), (BLOCKED, value_grads), (BLOCKED, map_grads), (WHOLE, after),
+            (LOOSE, next_mark), (BLOCKED, value_grads), (BLOCKED, map_grads), (WHOLE, after),
             (WHOLE, value_raw), (WHOLE, state_raw), (WHOLE, value_kernel), (WHOLE, state_kernel),
+            (LANES, gate_cross),
         ],
         [
             (BLOCKED, (count, channels), BF16),
             (BLOCKED, (count, maps_width), BF16),
             (WHOLE, (8, channels), F32),
             (WHOLE, (8, maps_width), F32),
+            (LANES, (8, count), F32),
         ],
         steps=chunks,
         backward=True,
@@ -1016,31 +1062,33 @@
     late_kept, late_given = run(
         late_kernel, "late", 3 * count * channels * width,
         [
-            core, (WHOLE, normed), (WHOLE, value_raw_grad), (WHOLE, state_raw_grad),
-            (WHOLE, value_small), (WHOLE, gate_small), (WHOLE, early_gain), (WHOLE, state_small),
-            (WHOLE, value_weight), (WHOLE, state_weight), (WHOLE, gain_full),
+            core, (feature_block, normed), (WHOLE, value_raw_grad), (WHOLE, state_raw_grad),
+            (WHOLE, value_small), (WHOLE, gate_small), (((1, BLOCK), lambda i: (0, i)), early_gain),
+            (WHOLE, state_small), (BLOCK, value_weight), (BLOCK, state_weight),
+            (((8, BLOCK), lambda i: (0, i)), gain_full),
         ],
         [(WHOLE, (chips, late_rows, channels), BF16)] * 2,
+        steps=features,
         scratch=[
             pltpu.VMEM((HALO, channels), F32),
             pltpu.VMEM((HALO, channels), F32),
             pltpu.VMEM((8, width), F32),
-            pltpu.VMEM((width, channels + maps_width), F32),
         ],
     )
     normed_parts = run(
-        normed_kernel, "normed", 4 * count * channels * width,
+        functools.partial(normed_kernel, chunks), "normed", 4 * count * channels * width,
         [
             (LOOSE, late_given), (WHOLE, gate_grad), (WHOLE, value_raw_grad),
-            (WHOLE, state_raw_grad), (WHOLE, gate_weight), (WHOLE, value_weight),
-            (WHOLE, state_weight), (WHOLE, full), (WHOLE, gain_full),
-        ],
-        [(WHOLE, (head_size, count + HALO, own_width), BF16)],
+            (WHOLE, state_raw_grad), (own_width, gate_weight), (own_width, value_weight),
+            (own_width, state_weight), (WHOLE, crossed),
+        ],
+        [(LEADING, (head_size, count + HALO, own_width), BF16)],
+        steps=head_size,
     )[0]
     normed_parts = deal(normed_parts, "head")
-    late_cut = step // 3 * 2 // 16 * 16
-    late_first, late_rest, _ = sum_pieces(chip, late_kept, late_given, late_cut, True, "late")
-    late_last, shared_piece = late_rest[: step - late_cut].astype(BF16), late_rest[step - late_cut :]
+    late_piece, shared_piece, _, _ = sum_pieces(
+        chip, late_kept, late_given, step, True, "late", False
+    )
     summed = butterfly(shared_piece, "head")
     line = jnp.arange(late_rows - step)[:, None]
     own_line = (line >= state_rows) & (line < state_rows + 2)
@@ -1065,8 +1113,8 @@
         [(step, (width, channels), F32), (out_rows, (channels, width), F32)], 4 * channels * width,
     )
     value_weight_gradient = unpack(
-        late_out_kernel, "late_out", [(late_first, (2, 1)), (late_last, (1, 2))],
-        [(step, (width, channels), F32)], 2 * channels * width, extra=(late_cut,),
+        late_out_kernel, "late_out", [(late_piece, None)],
+        [(step, (width, channels), F32)], 2 * channels * width,
     )[0]
     (
         state_weight_gradient, value_kernel_gradient, value_bias_gradient, state_kernel_gradient,

time: 313 us -> 324 us (1.035)
  Pallas kernels: 63.1 us -> 113 us
  starting transfers between devices: 105 us -> 75 us
  local copies, waits for them, and re-layouts: 45.9 us -> 22.2 us
  waiting for transfers between devices: 66.4 us -> 86.4 us
  other arithmetic: 18.3 us -> 12.7 us
    pallas_call x22, Pallas kernels: 63.1 us -> 113 us  [run(): pl.pallas_call(kernel, out_shape=shapes, in_specs=[spec(kind, a.shape) fo...]
    unnamed x183 -> x103, local copies, waits for them, and re-layouts: 36.6 us -> 14 us
    ppermute x16, starting transfers between devices: 33.8 us -> 17.6 us  [beside(): return lax.ppermute(value, 'core', [(0, 1), (1, 0)])]
    ppermute x2, waiting for transfers between devices: 9.28 us -> 21.9 us  [butterfly(): lax.ppermute(value, axis, [(i, i ^ bits) for i in range(size)])]
    ppermute x7 -> x4, starting transfers between devices: 14.8 us -> 5.69 us  [turn(): lax.ppermute(value, axis, [(i, (i + by) % size) for i in range(size)])]
    ppermute x1, waiting for transfers between devices: 0.01 us -> 8.95 us  [line_parts(): passed = lax.ppermute(two, axis, [(2, 3), (1, 0)])]
    ppermute x7 -> x4, waiting for transfers between devices: 8.59 us -> 1.65 us  [turn(): lax.ppermute(value, axis, [(i, (i + by) % size) for i in range(size)])]
    ppermute x2, starting transfers between devices: 6.08 us -> 1.53 us  [butterfly(): lax.ppermute(value, axis, [(i, i ^ bits) for i in range(size)])]
  transfers between devices with their start and end apart: 58 -> 53, of which waited for: 19 -> 25; matrix products, arithmetic and copies ran while one was open for 11% -> 6% of each run, Pallas kernels for 15% -> 25%
where the time goes in v1:
time: 324 us; the launch traced here: 322 us
  Pallas kernels  113 us (35%)
  waiting for transfers between devices  86.4 us (27%)
  starting transfers between devices  75 us (23%)
  local copies, waits for them, and re-layouts  22.2 us (7%)
  other arithmetic  12.7 us (4%)
  matrix products  11.8 us (4%)
    pallas_call x22, Pallas kernels, run(): pl.pallas_call(kernel, out_shape=shapes, in_specs=[spec(kind, a.shape) fo...  113 us
    ppermute x22, waiting for transfers between devices, cross(): lax.ppermute(value, 'chip', [(i, i ^ bits) for i in range(lax.axis_size('...  44.6 us
    ppermute x2, waiting for transfers between devices, butterfly(): lax.ppermute(value, axis, [(i, i ^ bits) for i in range(size)])  21.9 us
    ppermute x22, starting transfers between devices, cross(): lax.ppermute(value, 'chip', [(i, i ^ bits) for i in range(lax.axis_size('...  19.5 us
    ppermute x16, starting transfers between devices, beside(): return lax.ppermute(value, 'core', [(0, 1), (1, 0)])  17.6 us
    unnamed x103, local copies, waits for them, and re-layouts  14 us
    all_to_all x3, starting transfers between devices, deal(): return lax.all_to_all(parts, axis, 0, 0)  12.7 us
    ppermute x1, waiting for transfers between devices, line_parts(): passed = lax.ppermute(two, axis, [(2, 3), (1, 0)])  8.95 us
  transfers between devices with their start and end apart: 53, of which 25 were waited for; matrix products, arithmetic and copies ran while one was open for 6% of the time, Pallas kernels for 25%

profile of v1, /device:TPU:1, one launch (start us, length us, event | category | flops | bytes accessed | tf_op | source)
XLA Modules:
  0.0 321.8 jit_solution(4011431226362263308)
XLA Ops:
  1.4 4.5 %collective-permute-start = (bf16[16,384]{1,0:T(8,128)(2,1)S(1)}, bf16[16,384]{1,0:T(8,128)(2,1)S(1)}, u32[]{:S(2)}, u32[]{:S(2)}) collective-permute-start(bf16[16,384]{1,0:T(8,128)(2,1)S(1)} %slice_bitcast_fusion), channel_id=1, source_target_pairs={{0,4},{4,8},{8,12},{12,16},{16,20},{20,24},{24,28},{1,5},{5,9},{9,... | collective-permute-start | bytes 36872 | tf_op jit(solution)/shard_map/ppermute | solution.py:46
  12.6 4.6 %decays.1 = (f32[512,768]{1,0:T(8,128)}, f32[512,768]{1,0:T(8,128)}, f32[8,768]{1,0:T(8,128)}, f32[8,8,768]{2,1,0:T(8,128)}) custom-call(s32[512,12]{1,0:T(8,128)} %bitcast.34, f32[512,12]{1,0:T(8,128)} %negate_sqrt_fusion.weight_ref), custom_call_target="tpu_custom_call" | custom-call | flops 78643200 | bytes 3416064 | tf_op jit(solution)/shard_map/decays/pallas_call | solution.py:860
  17.2 5.2 %all-to-all-start = ((f32[8,8,768]{2,1,0:T(8,128)}), f32[8,8,768]{2,1,0:T(8,128)S(1)}, u32[]{:S(2)}, u32[]{:S(2)}) async-start(f32[8,8,768]{2,1,0:T(8,128)} %get-tuple-element.75), calls=%async_computation | async-start | bytes 393216 | tf_op jit(solution)/shard_map/all_to_all | solution.py:911
  34.6 3.8 %collective-permute-done.4.refs_3_.refs_7_ = bf16[544,384]{1,0:T(8,128)(2,1)S(1)} collective-permute-done((bf16[544,384]{1,0:T(8,128)(2,1)S(1)}, bf16[544,384]{1,0:T(8,128)(2,1)S(1)}, u32[]{:S(2)}, u32[]{:S(2)}) %collective-permute-start.4) | collective-permute-done | bytes 417824 | tf_op jit(solution)/shard_map/ppermute | solution.py:67
  38.4 9.0 %collective-permute-done.2.passed_ref.refs_8_ = bf16[544,384]{1,0:T(8,128)(2,1)S(1)} collective-permute-done((bf16[544,384]{1,0:T(8,128)(2,1)}, bf16[544,384]{1,0:T(8,128)(2,1)S(1)}, u32[]{:S(2)}, u32[]{:S(2)}) %collective-permute-start.2) | collective-permute-done | bytes 417824 | tf_op jit(solution)/shard_map/ppermute | solution.py:68
  48.1 3.8 %norm.1 = (bf16[544,1536]{1,0:T(8,128)(2,1)}, f32[544,128]{1,0:T(8,128)}, bf16[4,512,384]{2,1,0:T(8,128)(2,1)}, f32[8,1536]{1,0:T(8,128)}) custom-call(s32[1]{0:T(128)} %bitcast.3.head_ref, bf16[544,384]{1,0:T(8,128)(2,1)} %copy-done.17, bf16[544,384]{1,0:T(8,128)(2,1)} %copy-done.3, bf16[544,384]{1,0:T(8,128)(2,1)} %copy-done.15, ...), custom_call_target="tpu_custom_call" | custom-call | flops 7864320 | bytes 8142852 | tf_op jit(solution)/shard_map/norm/pallas_call | solution.py:860
  51.9 4.3 %all-to-all-start.1 = ((bf16[4,512,384]{2,1,0:T(8,128)(2,1)}), bf16[4,512,384]{2,1,0:T(8,128)(2,1)S(1)}, u32[]{:S(2)}, u32[]{:S(2)}) async-start(bf16[4,512,384]{2,1,0:T(8,128)(2,1)} %get-tuple-element.84), calls=%async_computation.1 | async-start | bytes 3145728 | tf_op jit(solution)/shard_map/all_to_all | solution.py:73
  62.5 6.5 %conv.1 = (bf16[512,768]{1,0:T(8,128)(2,1)}, bf16[512,768]{1,0:T(8,128)(2,1)}, f32[512,768]{1,0:T(8,128)}, bf16[512,256]{1,0:T(8,128)(2,1)}, f32[512,256]{1,0:T(8,128)}, /*index=5*/f32[128,768]{1,0:T(8,128)}) custom-call(bf16[544,768]{1,0:T(8,128)(2,1)} %convolution_convert_fusion.value_ref.value_raw_ref, ...), custom_call_target="tpu_custom_call" | custom-call | flops 157286400 | bytes 7047168 | tf_op jit(solution)/shard_map/conv/pallas_call | solution.py:860
  77.8 4.0 %collective-permute-done.6 = f32[64,768]{1,0:T(8,128)S(1)} collective-permute-done((f32[64,768]{1,0:T(8,128)S(1)}, f32[64,768]{1,0:T(8,128)S(1)}, u32[]{:S(2)}, u32[]{:S(2)}) %collective-permute-start.6) | collective-permute-done | bytes 196640 | tf_op jit(solution)/shard_map/ppermute | solution.py:77
  82.7 4.3 %collective-permute-done.8 = f32[64,768]{1,0:T(8,128)S(1)} collective-permute-done((f32[64,768]{1,0:T(8,128)S(1)}, f32[64,768]{1,0:T(8,128)S(1)}, u32[]{:S(2)}, u32[]{:S(2)}) %collective-permute-start.8) | collective-permute-done | bytes 196640 | tf_op jit(solution)/shard_map/ppermute | solution.py:77
  96.7 4.0 %fusion.3.grad_ref.refs_6_ = f32[512,768]{1,0:T(8,128)} fusion(bf16[512,1536]{1,0:T(8,128)(2,1)} %place.1.grad_ref, bf16[768,1536]{1,0:T(8,128)(2,1)S(1)} %copy-done.11), kind=kOutput, calls=%fused_computation.38 | convolution fusion | flops 1207959552 | bytes 5505024 | tf_op jit(solution)/shard_map/dot_general | solution.py:185
  100.7 6.0 %mixer.1 = (f32[512,768]{1,0:T(8,128)}, f32[8,512]{1,0:T(8,128)}, bf16[4,128,768]{2,1,0:T(8,128)(2,1)}, bf16[4,128,768]{2,1,0:T(8,128)(2,1)}) custom-call(f32[128,768]{1,0:T(8,128)} %add_select_fusion.1.state_in_ref, bf16[512,256]{1,0:T(8,128)(2,1)} %get-tuple-element.80.maps_ref.refs_11_, bf16[512,768]{1,0:T(8,128)(2,1)} %get-tuple-element.81.weighted_ref, ...), custom_call_target="tpu_custom_call" | custom-call | flops 393216000 | bytes 10138112 | tf_op jit(solution)/shard_map/mixer/pallas_call | solution.py:860
  112.3 6.5 %gate.1 = (bf16[512,768]{1,0:T(8,128)(2,1)}, bf16[512,768]{1,0:T(8,128)(2,1)}, f32[512,768]{1,0:T(8,128)}, f32[8,768]{1,0:T(8,128)}, f32[128,768]{1,0:T(8,128)}, /*index=5*/f32[8,512]{1,0:T(8,128)}) custom-call(f32[8,512]{1,0:T(8,128)} %get-tuple-element.85.refs_0_, f32[8,512]{1,0:T(8,128)} %copy-done.42, f32[8,512]{1,0:T(8,128)} %copy-done.43, ...), custom_call_target="tpu_custom_call" | custom-call | flops 235929600 | bytes 11011584 | tf_op jit(solution)/shard_map/gate/pallas_call | solution.py:860
  121.8 4.9 %out.1.refs_1_.out_ref = bf16[4,512,384]{2,1,0:T(8,128)(2,1)} custom-call(f32[128,768]{1,0:T(8,128)} %get-tuple-element.87.pair_ref, bf16[512,768]{1,0:T(8,128)(2,1)} %get-tuple-element.88.mixed_ref, bf16[768,1536]{1,0:T(8,128)(2,1)} %weight_ref.2), custom_call_target="tpu_custom_call" | custom-call | flops 1207959552 | bytes 4718592 | tf_op jit(solution)/shard_map/out/pallas_call | solution.py:860
  130.8 5.3 %collective-permute-done.14.loose_ref = f32[64,768]{1,0:T(8,128)S(1)} collective-permute-done((f32[64,768]{1,0:T(8,128)S(1)}, f32[64,768]{1,0:T(8,128)S(1)}, u32[]{:S(2)}, u32[]{:S(2)}) %collective-permute-start.14) | collective-permute-done | bytes 196640 | tf_op jit(solution)/shard_map/ppermute | solution.py:77
  136.8 9.6 %early.1 = (bf16[4,384,768]{2,1,0:T(8,128)(2,1)}, bf16[4,384,768]{2,1,0:T(8,128)(2,1)}, f32[1,1536]{1,0:T(1,128)}) custom-call(f32[64,768]{1,0:T(8,128)} %copy-done.38, s32[1]{0:T(128)} %bitcast.core_ref, bf16[544,1536]{1,0:T(8,128)(2,1)} %get-tuple-element.76.normed_ref, bf16[512,768]{1,0:T(8,128)(2,1)} %get-tuple-element.89.gate_ref.gate_grad_ref, ...), custom_call_target="tpu_custom_call" | custom-call | flops 2415919104 | bytes 11900932 | tf_op jit(solution)/shard_map/early/pallas_call | solution.py:860
  149.6 4.2 %all-to-all-start.2 = ((bf16[4,512,384]{2,1,0:T(8,128)(2,1)}), bf16[4,512,384]{2,1,0:T(8,128)(2,1)S(1)}, u32[]{:S(2)}, u32[]{:S(2)}) async-start(bf16[4,512,384]{2,1,0:T(8,128)(2,1)} %out.1.refs_1_.out_ref), calls=%async_computation.2 | async-start | bytes 3145728 | tf_op jit(solution)/shard_map/all_to_all | solution.py:73
  153.8 3.8 %collective-permute-done.28 = f32[64,768]{1,0:T(8,128)S(1)} collective-permute-done((f32[64,768]{1,0:T(8,128)S(1)}, f32[64,768]{1,0:T(8,128)S(1)}, u32[]{:S(2)}, u32[]{:S(2)}) %collective-permute-start.28) | collective-permute-done | bytes 196640 | tf_op jit(solution)/shard_map/ppermute | solution.py:77
  158.6 4.6 %early_half.1 = (f32[2,192,768]{2,1,0:T(8,128)}, bf16[2,192,768]{2,1,0:T(8,128)(2,1)}, f32[2,192,768]{2,1,0:T(8,128)}, bf16[2,192,768]{2,1,0:T(8,128)(2,1)}) custom-call(s32[1]{0:T(128)} %bitcast.1.chip_ref, bf16[4,384,768]{2,1,0:T(8,128)(2,1)} %get-tuple-element.90.kept_ref, bf16[4,384,768]{2,1,0:T(8,128)(2,1)} %collective-permute-done.15.arrived_ref), custom_call_target="tpu_custom_call" | custom-call | flops 1179648 | bytes 8257540 | tf_op jit(solution)/shard_map/early_half/pallas_call | solution.py:860
  165.6 8.6 %back.1 = (f32[512,768]{1,0:T(8,128)}, f32[512,256]{1,0:T(8,128)}) custom-call(f32[2,192,768]{2,1,0:T(8,128)} %get-tuple-element.92.first_ref.early_ref, bf16[4,512,384]{2,1,0:T(8,128)(2,1)} %out.1.refs_1_.out_ref, f32[128,768]{1,0:T(8,128)} %add_select_fusion.state_in_ref, f32[512,768]{1,0:T(8,128)} %get-tuple-element.103.mixer_grad_ref, ...), custom_call_target="tpu_custom_call" | custom-call | flops 786432000 | bytes 11955200 | tf_op jit(solution)/shard_map/back/pallas_call | solution.py:860
  184.2 5.9 %conv_back.1 = (bf16[512,768]{1,0:T(8,128)(2,1)}, bf16[512,256]{1,0:T(8,128)(2,1)}, f32[8,768]{1,0:T(8,128)}, f32[8,256]{1,0:T(8,128)}, f32[8,512]{1,0:T(8,128)}) custom-call(f32[192,768]{1,0:T(8,128)} %get-tuple-element.96.first_ref.other_ref, f32[512,768]{1,0:T(8,128)} %get-tuple-element.108.value_ref, f32[512,256]{1,0:T(8,128)} %get-tuple-element.109.map_ref, ...), custom_call_target="tpu_custom_call" | custom-call | flops 39321600 | bytes 4366336 | tf_op jit(solution)/shard_map/conv_back/pallas_call | solution.py:860
  190.0 7.8 %late.1 = (bf16[4,272,768]{2,1,0:T(8,128)(2,1)}, bf16[4,272,768]{2,1,0:T(8,128)(2,1)}) custom-call(s32[1]{0:T(128)} %bitcast.core_ref, bf16[544,1536]{1,0:T(8,128)(2,1)} %get-tuple-element.76.normed_ref, bf16[512,768]{1,0:T(8,128)(2,1)} %get-tuple-element.111.value_ref.value_grad_ref, bf16[512,256]{1,0:T(8,128)(2,1)} %get-tuple-element.112.state_ref.state_grad_ref, ...), custom_call_target="tpu_custom_call" | custom-call | flops 1811939328 | bytes 9320452 | tf_op jit(solution)/shard_map/late/pallas_call | solution.py:860
  200.5 7.7 %normed.1 = bf16[4,528,384]{2,1,0:T(8,128)(2,1)} custom-call(bf16[4,272,768]{2,1,0:T(8,128)(2,1)} %get-tuple-element.118.late_ref, bf16[512,768]{1,0:T(8,128)(2,1)} %get-tuple-element.89.gate_ref.gate_grad_ref, bf16[512,768]{1,0:T(8,128)(2,1)} %get-tuple-element.111.value_ref.value_grad_ref, bf16[512,256]{1,0:T(8,128)(2,1)} %get-tuple-element.112.state_ref.state_grad_ref, ...), custom_call_target="tpu_custom_call" | custom-call | flops 2415919104 | bytes 8978432 | tf_op jit(solution)/shard_map/normed/pallas_call | solution.py:860
  208.2 4.2 %all-to-all-start.3 = ((bf16[4,528,384]{2,1,0:T(8,128)(2,1)}), bf16[4,528,384]{2,1,0:T(8,128)(2,1)S(1)}, u32[]{:S(2)}, u32[]{:S(2)}) async-start(bf16[4,528,384]{2,1,0:T(8,128)(2,1)} %normed.1), calls=%async_computation.3 | async-start | bytes 3244032 | tf_op jit(solution)/shard_map/all_to_all | solution.py:73
  224.9 7.3 %collective-permute-done.33.refs_1_ = bf16[272,768]{1,0:T(8,128)(2,1)S(1)} collective-permute-done((bf16[272,768]{1,0:T(8,128)(2,1)}, bf16[272,768]{1,0:T(8,128)(2,1)S(1)}, u32[]{:S(2)}, u32[]{:S(2)}) %collective-permute-start.33) | collective-permute-done | bytes 417824 | tf_op jit(solution)/shard_map/ppermute | solution.py:77
  232.7 8.5 %collective-permute-done.35.refs_3_ = bf16[272,768]{1,0:T(8,128)(2,1)S(1)} collective-permute-done((bf16[272,768]{1,0:T(8,128)(2,1)}, bf16[272,768]{1,0:T(8,128)(2,1)S(1)}, u32[]{:S(2)}, u32[]{:S(2)}) %collective-permute-start.35) | collective-permute-done | bytes 417824 | tf_op jit(solution)/shard_map/ppermute | solution.py:77
  245.9 10.2 %collective-permute-done.36 = f32[80,768]{1,0:T(8,128)S(1)} collective-permute-done((f32[80,768]{1,0:T(8,128)}, f32[80,768]{1,0:T(8,128)S(1)}, u32[]{:S(2)}, u32[]{:S(2)}) %collective-permute-start.36) | collective-permute-done | bytes 245792 | tf_op jit(solution)/shard_map/ppermute | solution.py:88
  258.6 11.7 %collective-permute-done.37 = f32[80,768]{1,0:T(8,128)S(1)} collective-permute-done((f32[80,768]{1,0:T(8,128)S(1)}, f32[80,768]{1,0:T(8,128)S(1)}, u32[]{:S(2)}, u32[]{:S(2)}) %collective-permute-start.37) | collective-permute-done | bytes 245792 | tf_op jit(solution)/shard_map/ppermute | solution.py:88
  282.2 5.3 %collective-permute-done.45 = bf16[192,768]{1,0:T(8,128)(2,1)} collective-permute-done((bf16[192,768]{1,0:T(8,128)(2,1)}, bf16[192,768]{1,0:T(8,128)(2,1)}, u32[]{:S(2)}, u32[]{:S(2)}) %collective-permute-start.45) | collective-permute-done | bytes 294944 | tf_op jit(solution)/shard_map/ppermute | solution.py:77
  293.7 7.4 %early_out.1 = (f32[1536,768]{1,0:T(8,128)}, f32[768,1536]{1,0:T(8,128)}) custom-call(s32[1]{0:T(128)} %bitcast.core_ref, s32[1]{0:T(128)} %bitcast.1.chip_ref, bf16[2,192,768]{2,1,0:T(8,128)(2,1)} %copy-done.10, bf16[2,192,768]{2,1,0:T(8,128)(2,1)} %copy-done.25, bf16[2,192,768]{2,1,0:T(8,128)(2,1)} %copy-done.23, bf16[2,192,768]{2,1,0:T(8,128)(2,1)} %copy-done.27, ...), custom_call_target="tpu_custom_call" | custom-call | flops 4718592 | bytes 14155784 | tf_op jit(solution)/shard_map/early_out/pallas_call | solution.py:860
  305.3 5.4 %late_out.1 = f32[1536,768]{1,0:T(8,128)} custom-call(s32[1]{0:T(128)} %bitcast.core_ref, s32[1]{0:T(128)} %bitcast.1.chip_ref, bf16[1,192,768]{2,1,0:T(8,128)(2,1)} %bitcast.15.refs_0_, bf16[1,192,768]{2,1,0:T(8,128)(2,1)} %collective-permute-done.42.refs_1_, bf16[1,192,768]{2,1,0:T(8,128)(2,1)} %bitcast.16.refs_2_, ...), custom_call_target="tpu_custom_call" | custom-call | flops 2359296 | bytes 7077896 | tf_op jit(solution)/shard_map/late_out/pallas_call | solution.py:860
  312.1 4.5 %shared_out.1 = (f32[1536,256]{1,0:T(8,128)}, f32[4,768]{1,0:T(4,128)}, f32[1,768]{1,0:T(1,128)}, f32[4,256]{1,0:T(4,128)}, f32[1,256]{1,0:T(1,128)}, /*index=5*...) custom-call(s32[1]{0:T(128)} %bitcast.core_ref, s32[1]{0:T(128)} %bitcast.1.chip_ref, bf16[2,80,768]{2,1,0:T(8,128)(2,1)} %copy-done.18, ...), custom_call_target="tpu_custom_call" | custom-call | flops 786432 | bytes 2588680 | tf_op jit(solution)/shard_map/shared_out/pallas_call | solution.py:860
  (243 shorter events, 127.3 us)
Async XLA Ops:
  8.4 21.5 %collective-permute-start.1 = (bf16[544,384]{1,0:T(8,128)(2,1)S(1)}, bf16[544,384]{1,0:T(8,128)(2,1)S(1)}, u32[]{:S(2)}, u32[]{:S(2)}) collective-permute-start(bf16[544,384]{1,0:T(8,128)(2,1)S(1)} %pad_maximum_fusion.2.refs_0_.refs_4_), channel_id=1, source_target_pairs={{0,2},{1,3},{2,0},{3,1},{4,6},{5,7},{6,4},{7,5},{8,10},{9,11},{10,... | collective-permute-start | bytes 1253384 | tf_op jit(solution)/shard_map/ppermute | solution.py:55
  22.4 12.3 %collective-permute-start.3 = (bf16[544,384]{1,0:T(8,128)(2,1)S(1)}, bf16[544,384]{1,0:T(8,128)(2,1)S(1)}, u32[]{:S(2)}, u32[]{:S(2)}) collective-permute-start(bf16[544,384]{1,0:T(8,128)(2,1)S(1)} %pad_maximum_fusion.2.refs_0_.refs_4_), channel_id=1, source_target_pairs={{0,1},{1,2},{2,3},{4,5},{5,6},{6,7},{8,9},{9,10},{10,11},{12,13},{... | collective-permute-start | bytes 1253384 | tf_op jit(solution)/shard_map/ppermute | solution.py:66
  25.6 12.8 %collective-permute-start.4 = (bf16[544,384]{1,0:T(8,128)(2,1)S(1)}, bf16[544,384]{1,0:T(8,128)(2,1)S(1)}, u32[]{:S(2)}, u32[]{:S(2)}) collective-permute-start(bf16[544,384]{1,0:T(8,128)(2,1)S(1)} %pad_maximum_fusion.2.refs_0_.refs_4_), channel_id=1, source_target_pairs={{1,0},{2,1},{3,2},{5,4},{6,5},{7,6},{9,8},{10,9},{11,10},{13,12},{... | collective-permute-start | bytes 1253384 | tf_op jit(solution)/shard_map/ppermute | solution.py:67
  30.7 16.7 %collective-permute-start.2 = (bf16[544,384]{1,0:T(8,128)(2,1)}, bf16[544,384]{1,0:T(8,128)(2,1)S(1)}, u32[]{:S(2)}, u32[]{:S(2)}) collective-permute-start(bf16[544,384]{1,0:T(8,128)(2,1)} %tie.3.refs_2_.refs_6_), channel_id=1, source_target_pairs={{2,3},{1,0},{6,7},{5,4},{10,11},{9,8},{14,15},{13,12},{18,19},{17,... | collective-permute-start | bytes 1253384 | tf_op jit(solution)/shard_map/ppermute | solution.py:68
  51.9 40.8 %all-to-all-start.1 = ((bf16[4,512,384]{2,1,0:T(8,128)(2,1)}), bf16[4,512,384]{2,1,0:T(8,128)(2,1)S(1)}, u32[]{:S(2)}, u32[]{:S(2)}) async-start(bf16[4,512,384]{2,1,0:T(8,128)(2,1)} %get-tuple-element.84), calls=%async_computation.1 | async-start | bytes 3145728 | tf_op jit(solution)/shard_map/all_to_all | solution.py:73
  146.3 12.3 %collective-permute-start.15 = (bf16[4,384,768]{2,1,0:T(8,128)(2,1)}, bf16[4,384,768]{2,1,0:T(8,128)(2,1)}, u32[]{:S(2)}, u32[]{:S(2)}) collective-permute-start(bf16[4,384,768]{2,1,0:T(8,128)(2,1)} %get-tuple-element.91), channel_id=1, source_target_pairs={{0,4},{4,0},{1,5},{5,1},{2,6},{6,2},{3,7},{7,3},{8,12},{12,8},{9,1... | collective-permute-start | bytes 7077896 | tf_op jit(solution)/shard_map/ppermute | solution.py:50
  149.6 58.6 %all-to-all-start.2 = ((bf16[4,512,384]{2,1,0:T(8,128)(2,1)}), bf16[4,512,384]{2,1,0:T(8,128)(2,1)S(1)}, u32[]{:S(2)}, u32[]{:S(2)}) async-start(bf16[4,512,384]{2,1,0:T(8,128)(2,1)} %out.1.refs_1_.out_ref), calls=%async_computation.2 | async-start | bytes 3145728 | tf_op jit(solution)/shard_map/all_to_all | solution.py:73
  163.3 15.1 %collective-permute-start.16 = (bf16[2,192,768]{2,1,0:T(8,128)(2,1)}, bf16[2,192,768]{2,1,0:T(8,128)(2,1)S(1)}, u32[]{:S(2)}, u32[]{:S(2)}) collective-permute-start(bf16[2,192,768]{2,1,0:T(8,128)(2,1)} %get-tuple-element.93), channel_id=1, source_target_pairs={{0,8},{8,0},{16,24},{24,16},{1,9},{9,1},{17,25},{25,17},{2,10},{10... | collective-permute-start | bytes 1769480 | tf_op jit(solution)/shard_map/ppermute | solution.py:77
  164.7 14.8 %collective-permute-start.17 = (bf16[2,192,768]{2,1,0:T(8,128)(2,1)}, bf16[2,192,768]{2,1,0:T(8,128)(2,1)S(1)}, u32[]{:S(2)}, u32[]{:S(2)}) collective-permute-start(bf16[2,192,768]{2,1,0:T(8,128)(2,1)} %get-tuple-element.95), channel_id=1, source_target_pairs={{0,16},{8,24},{16,0},{24,8},{1,17},{9,25},{17,1},{25,9},{2,18},{10... | collective-permute-start | bytes 1769480 | tf_op jit(solution)/shard_map/ppermute | solution.py:77
  197.9 19.0 %collective-permute-start.32 = (bf16[4,272,768]{2,1,0:T(8,128)(2,1)}, bf16[4,272,768]{2,1,0:T(8,128)(2,1)}, u32[]{:S(2)}, u32[]{:S(2)}) collective-permute-start(bf16[4,272,768]{2,1,0:T(8,128)(2,1)} %get-tuple-element.118.late_ref), channel_id=1, source_target_pairs={{0,4},{4,0},{1,5},{5,1},{2,6},{6,2},{3,7},{7,3},{8,12},{12,8},{9,1... | collective-permute-start | bytes 5013512 | tf_op jit(solution)/shard_map/ppermute | solution.py:50
  199.0 13.4 %collective-permute-start.18 = (bf16[192,768]{1,0:T(8,128)(2,1)}, bf16[192,768]{1,0:T(8,128)(2,1)S(1)}, u32[]{:S(2)}, u32[]{:S(2)}) collective-permute-start(bf16[192,768]{1,0:T(8,128)(2,1)} %get-tuple-element.97), channel_id=1, source_target_pairs={{0,16},{8,24},{16,0},{24,8},{1,17},{9,25},{17,1},{25,9},{2,18},{10... | collective-permute-start | bytes 884744 | tf_op jit(solution)/shard_map/ppermute | solution.py:77
  199.2 13.2 %collective-permute-start.19 = (bf16[192,768]{1,0:T(8,128)(2,1)}, bf16[192,768]{1,0:T(8,128)(2,1)}, u32[]{:S(2)}, u32[]{:S(2)}) collective-permute-start(bf16[192,768]{1,0:T(8,128)(2,1)} %get-tuple-element.99), channel_id=1, source_target_pairs={{0,8},{8,0},{16,24},{24,16},{1,9},{9,1},{17,25},{25,17},{2,10},{10... | collective-permute-start | bytes 884744 | tf_op jit(solution)/shard_map/ppermute | solution.py:77
  208.2 93.0 %all-to-all-start.3 = ((bf16[4,528,384]{2,1,0:T(8,128)(2,1)}), bf16[4,528,384]{2,1,0:T(8,128)(2,1)S(1)}, u32[]{:S(2)}, u32[]{:S(2)}) async-start(bf16[4,528,384]{2,1,0:T(8,128)(2,1)} %normed.1), calls=%async_computation.3 | async-start | bytes 3244032 | tf_op jit(solution)/shard_map/all_to_all | solution.py:73
  220.3 11.9 %collective-permute-start.33 = (bf16[272,768]{1,0:T(8,128)(2,1)}, bf16[272,768]{1,0:T(8,128)(2,1)S(1)}, u32[]{:S(2)}, u32[]{:S(2)}) collective-permute-start(bf16[272,768]{1,0:T(8,128)(2,1)} %get-tuple-element.123), channel_id=1, source_target_pairs={{0,8},{8,0},{16,24},{24,16},{1,9},{9,1},{17,25},{25,17},{2,10},{10... | collective-permute-start | bytes 1253384 | tf_op jit(solution)/shard_map/ppermute | solution.py:77
  220.5 12.2 %collective-permute-start.34 = (bf16[272,768]{1,0:T(8,128)(2,1)}, bf16[272,768]{1,0:T(8,128)(2,1)S(1)}, u32[]{:S(2)}, u32[]{:S(2)}) collective-permute-start(bf16[272,768]{1,0:T(8,128)(2,1)} %get-tuple-element.124), channel_id=1, source_target_pairs={{0,16},{8,24},{16,0},{24,8},{1,17},{9,25},{17,1},{25,9},{2,18},{10... | collective-permute-start | bytes 1253384 | tf_op jit(solution)/shard_map/ppermute | solution.py:77
  221.9 19.4 %collective-permute-start.35 = (bf16[272,768]{1,0:T(8,128)(2,1)}, bf16[272,768]{1,0:T(8,128)(2,1)S(1)}, u32[]{:S(2)}, u32[]{:S(2)}) collective-permute-start(bf16[272,768]{1,0:T(8,128)(2,1)} %get-tuple-element.125), channel_id=1, source_target_pairs={{0,24},{8,16},{16,8},{24,0},{1,25},{9,17},{17,9},{25,1},{2,26},{10... | collective-permute-start | bytes 1253384 | tf_op jit(solution)/shard_map/ppermute | solution.py:77
  223.3 34.6 %collective-permute-start.26 = (bf16[2,192,768]{2,1,0:T(8,128)(2,1)S(1)}, bf16[2,192,768]{2,1,0:T(8,128)(2,1)S(1)}, u32[]{:S(2)}, u32[]{:S(2)}) collective-permute-start(bf16[2,192,768]{2,1,0:T(8,128)(2,1)S(1)} %pad_maximum_fusion.1.refs_4_), channel_id=1, source_target_pairs={{0,16},{8,24},{16,0},{24,8},{1,17},{9,25},{17,1},{25,9},{2,18},{10... | collective-permute-start | bytes 1769480 | tf_op jit(solution)/shard_map/ppermute | solution.py:77
  223.6 34.8 %collective-permute-start.22 = (bf16[2,192,768]{2,1,0:T(8,128)(2,1)S(1)}, bf16[2,192,768]{2,1,0:T(8,128)(2,1)S(1)}, u32[]{:S(2)}, u32[]{:S(2)}) collective-permute-start(bf16[2,192,768]{2,1,0:T(8,128)(2,1)S(1)} %pad_maximum_fusion.refs_0_), channel_id=1, source_target_pairs={{0,8},{8,0},{16,24},{24,16},{1,9},{9,1},{17,25},{25,17},{2,10},{10... | collective-permute-start | bytes 1769480 | tf_op jit(solution)/shard_map/ppermute | solution.py:77
  257.1 13.2 %collective-permute-start.37 = (f32[80,768]{1,0:T(8,128)S(1)}, f32[80,768]{1,0:T(8,128)S(1)}, u32[]{:S(2)}, u32[]{:S(2)}) collective-permute-start(f32[80,768]{1,0:T(8,128)S(1)} %add.68), channel_id=1, source_target_pairs={{0,2},{1,3},{2,0},{3,1},{4,6},{5,7},{6,4},{7,5},{8,10},{9,11},{10,... | collective-permute-start | bytes 737288 | tf_op jit(solution)/shard_map/ppermute | solution.py:88
  257.1 14.3 %collective-permute-start.25 = (bf16[2,192,768]{2,1,0:T(8,128)(2,1)S(1)}, bf16[2,192,768]{2,1,0:T(8,128)(2,1)S(1)}, u32[]{:S(2)}, u32[]{:S(2)}) collective-permute-start(bf16[2,192,768]{2,1,0:T(8,128)(2,1)S(1)} %pad_maximum_fusion.1.refs_4_), channel_id=1, source_target_pairs={{0,4},{4,0},{1,5},{5,1},{2,6},{6,2},{3,7},{7,3},{8,12},{12,8},{9,1... | collective-permute-start | bytes 1769480 | tf_op jit(solution)/shard_map/ppermute | solution.py:50
  257.9 15.1 %collective-permute-start.21 = (bf16[2,192,768]{2,1,0:T(8,128)(2,1)S(1)}, bf16[2,192,768]{2,1,0:T(8,128)(2,1)S(1)}, u32[]{:S(2)}, u32[]{:S(2)}) collective-permute-start(bf16[2,192,768]{2,1,0:T(8,128)(2,1)S(1)} %pad_maximum_fusion.refs_0_), channel_id=1, source_target_pairs={{0,4},{4,0},{1,5},{5,1},{2,6},{6,2},{3,7},{7,3},{8,12},{12,8},{9,1... | collective-permute-start | bytes 1769480 | tf_op jit(solution)/shard_map/ppermute | solution.py:50
  257.9 15.1 %collective-permute-start.27 = (bf16[2,192,768]{2,1,0:T(8,128)(2,1)S(1)}, bf16[2,192,768]{2,1,0:T(8,128)(2,1)S(1)}, u32[]{:S(2)}, u32[]{:S(2)}) collective-permute-start(bf16[2,192,768]{2,1,0:T(8,128)(2,1)S(1)} %collective-permute-done.26.refs_6_), channel_id=1, source_target_pairs={{0,4},{4,0},{1,5},{5,1},{2,6},{6,2},{3,7},{7,3},{8,12},{12,8},{9,1... | collective-permute-start | bytes 1769480 | tf_op jit(solution)/shard_map/ppermute | solution.py:50
  258.4 19.8 %collective-permute-start.23 = (bf16[2,192,768]{2,1,0:T(8,128)(2,1)S(1)}, bf16[2,192,768]{2,1,0:T(8,128)(2,1)S(1)}, u32[]{:S(2)}, u32[]{:S(2)}) collective-permute-start(bf16[2,192,768]{2,1,0:T(8,128)(2,1)S(1)} %collective-permute-done.22.refs_2_), channel_id=1, source_target_pairs={{0,4},{4,0},{1,5},{5,1},{2,6},{6,2},{3,7},{7,3},{8,12},{12,8},{9,1... | collective-permute-start | bytes 1769480 | tf_op jit(solution)/shard_map/ppermute | solution.py:50
  272.9 14.6 %collective-permute-start.45 = (bf16[192,768]{1,0:T(8,128)(2,1)}, bf16[192,768]{1,0:T(8,128)(2,1)}, u32[]{:S(2)}, u32[]{:S(2)}) collective-permute-start(bf16[192,768]{1,0:T(8,128)(2,1)} %get-tuple-element.128), channel_id=1, source_target_pairs={{0,16},{8,24},{16,0},{24,8},{1,17},{9,25},{17,1},{25,9},{2,18},{10... | collective-permute-start | bytes 884744 | tf_op jit(solution)/shard_map/ppermute | solution.py:77
  273.0 16.8 %collective-permute-start.47 = (bf16[192,768]{1,0:T(8,128)(2,1)}, bf16[192,768]{1,0:T(8,128)(2,1)}, u32[]{:S(2)}, u32[]{:S(2)}) collective-permute-start(bf16[192,768]{1,0:T(8,128)(2,1)} %get-tuple-element.128), channel_id=1, source_target_pairs={{0,24},{8,16},{16,8},{24,0},{1,25},{9,17},{17,9},{25,1},{2,26},{10... | collective-permute-start | bytes 884744 | tf_op jit(solution)/shard_map/ppermute | solution.py:77
  276.0 14.3 %collective-permute-start.42 = (bf16[1,192,768]{2,1,0:T(8,128)(2,1)}, bf16[1,192,768]{2,1,0:T(8,128)(2,1)}, u32[]{:S(2)}, u32[]{:S(2)}) collective-permute-start(bf16[1,192,768]{2,1,0:T(8,128)(2,1)} %bitcast.15.refs_0_), channel_id=1, source_target_pairs={{0,4},{4,0},{1,5},{5,1},{2,6},{6,2},{3,7},{7,3},{8,12},{12,8},{9,1... | collective-permute-start | bytes 884744 | tf_op jit(solution)/shard_map/ppermute | solution.py:50
  278.2 13.4 %collective-permute-start.40 = (bf16[2,80,768]{2,1,0:T(8,128)(2,1)S(1)}, bf16[2,80,768]{2,1,0:T(8,128)(2,1)}, u32[]{:S(2)}, u32[]{:S(2)}) collective-permute-start(bf16[2,80,768]{2,1,0:T(8,128)(2,1)S(1)} %pad_maximum_fusion.3.refs_0_), channel_id=1, source_target_pairs={{0,8},{8,0},{16,24},{24,16},{1,9},{9,1},{17,25},{25,17},{2,10},{10... | collective-permute-start | bytes 737288 | tf_op jit(solution)/shard_map/ppermute | solution.py:77
  279.9 25.3 %collective-permute-start.44 = (bf16[1,192,768]{2,1,0:T(8,128)(2,1)}, bf16[1,192,768]{2,1,0:T(8,128)(2,1)}, u32[]{:S(2)}, u32[]{:S(2)}) collective-permute-start(bf16[1,192,768]{2,1,0:T(8,128)(2,1)} %bitcast.16.refs_2_), channel_id=1, source_target_pairs={{0,4},{4,0},{1,5},{5,1},{2,6},{6,2},{3,7},{7,3},{8,12},{12,8},{9,1... | collective-permute-start | bytes 884744 | tf_op jit(solution)/shard_map/ppermute | solution.py:50
  287.5 17.8 %collective-permute-start.46 = (bf16[1,192,768]{2,1,0:T(8,128)(2,1)}, bf16[1,192,768]{2,1,0:T(8,128)(2,1)}, u32[]{:S(2)}, u32[]{:S(2)}) collective-permute-start(bf16[1,192,768]{2,1,0:T(8,128)(2,1)} %bitcast.17.refs_4_), channel_id=1, source_target_pairs={{0,4},{4,0},{1,5},{5,1},{2,6},{6,2},{3,7},{7,3},{8,12},{12,8},{9,1... | collective-permute-start | bytes 884744 | tf_op jit(solution)/shard_map/ppermute | solution.py:50
  289.9 15.4 %collective-permute-start.48 = (bf16[1,192,768]{2,1,0:T(8,128)(2,1)}, bf16[1,192,768]{2,1,0:T(8,128)(2,1)}, u32[]{:S(2)}, u32[]{:S(2)}) collective-permute-start(bf16[1,192,768]{2,1,0:T(8,128)(2,1)} %bitcast.18.refs_6_), channel_id=1, source_target_pairs={{0,4},{4,0},{1,5},{5,1},{2,6},{6,2},{3,7},{7,3},{8,12},{12,8},{9,1... | collective-permute-start | bytes 884744 | tf_op jit(solution)/shard_map/ppermute | solution.py:50
  290.2 20.4 %collective-permute-start.39 = (bf16[2,80,768]{2,1,0:T(8,128)(2,1)S(1)}, bf16[2,80,768]{2,1,0:T(8,128)(2,1)S(1)}, u32[]{:S(2)}, u32[]{:S(2)}) collective-permute-start(bf16[2,80,768]{2,1,0:T(8,128)(2,1)S(1)} %pad_maximum_fusion.3.refs_0_), channel_id=1, source_target_pairs={{0,4},{4,0},{1,5},{5,1},{2,6},{6,2},{3,7},{7,3},{8,12},{12,8},{9,1... | collective-permute-start | bytes 737288 | tf_op jit(solution)/shard_map/ppermute | solution.py:50
  291.6 19.1 %collective-permute-start.41 = (bf16[2,80,768]{2,1,0:T(8,128)(2,1)}, bf16[2,80,768]{2,1,0:T(8,128)(2,1)S(1)}, u32[]{:S(2)}, u32[]{:S(2)}) collective-permute-start(bf16[2,80,768]{2,1,0:T(8,128)(2,1)} %collective-permute-done.40.refs_2_), channel_id=1, source_target_pairs={{0,4},{4,0},{1,5},{5,1},{2,6},{6,2},{3,7},{7,3},{8,12},{12,8},{9,1... | collective-permute-start | bytes 737288 | tf_op jit(solution)/shard_map/ppermute | solution.py:50
  (72 other events, 594.5 us)
